TPU v7x, 32 devices: a whole 2x2x4 slice. The times are simulated.
32 devices in a mesh: seq: 8 (over z, y), head: 4 (over x, core).
Axes of the slice: x: 2, y: 2, z: 4, core: 2. Of those that a mesh axis runs over, the one named last changes fastest.
Arguments:
- queries: bfloat16 [4096, 2048], P('seq', 'head'), may hold values from -6 to 6
- key_vectors: bfloat16 [4096, 2048], P('seq', 'head'), may hold values from -6 to 6
- values: bfloat16 [4096, 4096], P('seq', 'head'), may hold values from -24 to 24
- gate_log: float32 [32, 4096], P('head', 'seq'), may hold values from -1 to 0
- write_rate: float32 [32, 4096], P('head', 'seq'), as said below
- prompt_stretches: int32 [4], replicated, may hold values from 1 to 32, as said below
- decode_owner: int32 [4], replicated, may hold values from 0 to 7, as said below
- norm_gain: float32 [128], replicated, may hold values from 0.25 to 1.75
- out_weight: bfloat16 [4096, 2048], P('head'), may hold values from -0.09375 to 0.09375
Outputs:
- mixed: bfloat16 [4096, 2048], P('seq', 'head')
- decode_states: float32 [8, 32, 128, 128], P('seq', 'head')
Inputs may be any that keep to these rules, and one draw needn't show every extreme that they name: `prompt_stretches`: prompts lie in order along the token dimension, each a whole number of stretches of 64 tokens; the lengths sum to 64 and the longest is exactly 32. `decode_owner`: the 4 entries are distinct. `write_rate`: every entry is positive.
All inputs are finite; a program needn't handle non-finite values.
Results may differ from a plain program's by a relative error of at most 0.014.
Values may be sent and summed in bfloat16 or wider, within the bound.
A program may use at most 64 MiB of HBM per device.

v0:
```python
from functools import partial

import jax
import jax.numpy as jnp
from jax import lax
from jax.sharding import PartitionSpec as P

DK = 128
DV = 128
STRETCH = 64


HIGH = lax.Precision.HIGHEST


def passed_along(block, axis, distance):
    devices = range(lax.axis_size(axis))
    route = [(i - distance, i) for i in devices if i - distance in devices]
    return lax.ppermute(block, axis, route)


def unit_rows(vectors):
    return vectors * lax.rsqrt(jnp.sum(vectors * vectors, axis=-1, keepdims=True) + 1e-06)


def stretch_terms(query_part, key_part, value_part, gate_part, rate_part):
    length = gate_part.shape[-1]
    cumulative = jnp.cumsum(gate_part, axis=-1)
    row_index = lax.broadcasted_iota(jnp.int32, (length, length), 0)
    col_index = lax.broadcasted_iota(jnp.int32, (length, length), 1)
    spread = cumulative[:, :, None] - cumulative[:, None, :]
    strict = jnp.exp(jnp.where(row_index > col_index, spread, -jnp.inf))
    causal = jnp.exp(jnp.where(row_index >= col_index, spread, -jnp.inf))
    key_gram = jnp.einsum("hid,hjd->hij", key_part, key_part, precision=HIGH)
    system = jnp.eye(length, dtype=jnp.float32) + rate_part[:, :, None] * key_gram * strict
    growth = jnp.exp(cumulative)
    targets = jnp.concatenate(
        [rate_part[:, :, None] * key_part * growth[:, :, None], rate_part[:, :, None] * value_part],
        axis=-1,
    )
    solved = jax.scipy.linalg.solve_triangular(system, targets, lower=True, unit_diagonal=True)
    width = key_part.shape[-1]
    key_mix = solved[..., :width]
    fresh_base = solved[..., width:]
    scores = jnp.einsum("hid,hjd->hij", query_part, key_part, precision=HIGH) * causal
    query_decay = query_part * growth[:, :, None]
    key_decay = key_part * jnp.exp(cumulative[:, -1:] - cumulative)[:, :, None]
    retain = jnp.exp(cumulative[:, -1])
    return (key_mix, fresh_base, scores, query_decay, key_decay, retain)


def stretch_inputs(query_rows, key_rows, value_rows, gate_rows, rate_rows, repeat):
    length = query_rows.shape[0]
    query_part = unit_rows(query_rows.astype(jnp.float32).reshape(length, -1, DK)) * DK ** (-0.5)
    key_part = unit_rows(key_rows.astype(jnp.float32).reshape(length, -1, DK))
    query_part = jnp.repeat(query_part, repeat, axis=1).transpose(1, 0, 2)
    key_part = jnp.repeat(key_part, repeat, axis=1).transpose(1, 0, 2)
    value_part = value_rows.astype(jnp.float32).reshape(length, -1, DV).transpose(1, 0, 2)
    return stretch_terms(query_part, key_part, value_part, gate_rows, rate_rows)


def head_norm(output, norm_gain):
    scaled = (
        output * lax.rsqrt(jnp.mean(output * output, axis=-1, keepdims=True) + 1e-06) * norm_gain
    )
    return scaled.astype(jnp.bfloat16)


def prompt_layout(prompt_stretches, stretch_ids):
    finish = jnp.cumsum(prompt_stretches)
    begin = finish - prompt_stretches
    opens = jnp.any(stretch_ids[:, None] == begin[None, :], axis=1)
    closes = jnp.any(stretch_ids[:, None] + 1 == finish[None, :], axis=1)
    owner_prompt = jnp.sum((finish[None, :] <= stretch_ids[:, None]).astype(jnp.int32), axis=1)
    return (finish, opens, closes, owner_prompt)


def addressed(closing_states, decode_owner, finish, position, number, devices_seq):
    owner_table = (
        decode_owner[:, None] == jnp.arange(devices_seq, dtype=jnp.int32)[None, :]
    ).astype(jnp.int32)
    assigned = jnp.sum(owner_table, axis=0) > 0
    last_stretch = jnp.sum(owner_table * (finish - 1)[:, None], axis=0)
    local_index = last_stretch - position * number
    present = assigned & (local_index >= 0) & (local_index < number)
    picked = jnp.take(closing_states, jnp.clip(local_index, 0, number - 1), axis=0)
    return jnp.where(present[:, None, None, None], picked, 0.0)


def body(
    queries,
    key_vectors,
    values,
    gate_log,
    write_rate,
    prompt_stretches,
    decode_owner,
    norm_gain,
    out_weight,
):
    local_rows = queries.shape[0]
    number = local_rows // STRETCH
    heads_here = gate_log.shape[0]
    repeat = heads_here // (queries.shape[1] // DK)
    position = lax.axis_index("seq")
    devices_seq = lax.axis_size("seq")
    stretch_ids = position * number + jnp.arange(number, dtype=jnp.int32)
    finish, opens, closes, owner_prompt = prompt_layout(prompt_stretches, stretch_ids)
    query_blocks = queries.reshape(number, STRETCH, -1)
    key_blocks = key_vectors.reshape(number, STRETCH, -1)
    value_blocks = values.reshape(number, STRETCH, -1)
    gate_blocks = gate_log.reshape(heads_here, number, STRETCH).transpose(1, 0, 2)
    rate_blocks = write_rate.reshape(heads_here, number, STRETCH).transpose(1, 0, 2)
    key_mix, fresh_base, scores, query_decay, key_decay, retain = jax.vmap(
        partial(stretch_inputs, repeat=repeat)
    )(query_blocks, key_blocks, value_blocks, gate_blocks, rate_blocks)
    identity = jnp.broadcast_to(jnp.eye(DK, dtype=jnp.float32), (heads_here, DK, DK))
    empty_state = jnp.zeros((heads_here, DK, DV), jnp.float32)

    def walk(carry, inputs):
        state, carried = carry
        mix_rows, base_rows, keep, decay_rows, opening = inputs
        state = jnp.where(opening, 0.0, state)
        carried = jnp.where(opening, 0.0, carried)
        fresh = base_rows - jnp.einsum("hcd,hde->hce", mix_rows, state, precision=HIGH)
        following = keep[:, None, None] * state + jnp.einsum(
            "hcd,hce->hde", decay_rows, fresh, precision=HIGH
        )
        pulled = jnp.einsum("hcd,hde->hce", mix_rows, carried, precision=HIGH)
        moved = keep[:, None, None] * carried - jnp.einsum(
            "hcd,hce->hde", decay_rows, pulled, precision=HIGH
        )
        return ((following, moved), (state, carried))

    (local_state, local_map), (start_states, start_maps) = lax.scan(
        walk, (empty_state, identity), (key_mix, fresh_base, retain, key_decay, opens)
    )

    def relay(turn, arriving):
        outgoing = jnp.einsum("hde,hef->hdf", local_map, arriving, precision=HIGH) + local_state
        return passed_along(outgoing, "seq", 1)

    incoming = lax.fori_loop(0, devices_seq - 1, relay, empty_state)
    starts = start_states + jnp.einsum("nhde,hef->nhdf", start_maps, incoming, precision=HIGH)
    fresh = fresh_base - jnp.einsum("nhcd,nhde->nhce", key_mix, starts, precision=HIGH)
    output = jnp.einsum("nhcd,nhde->nhce", query_decay, starts, precision=HIGH) + jnp.einsum(
        "nhij,nhje->nhie", scores, fresh, precision=HIGH
    )
    closing_states = retain[..., None, None] * starts + jnp.einsum(
        "nhcd,nhce->nhde", key_decay, fresh, precision=HIGH
    )
    outbound = addressed(closing_states, decode_owner, finish, position, number, devices_seq)
    arrived = lax.all_to_all(outbound[:, None], "seq", split_axis=0, concat_axis=1, tiled=True)
    owned = jnp.sum(arrived, axis=1)
    hidden = head_norm(output, norm_gain).transpose(0, 2, 1, 3).reshape(local_rows, heads_here * DV)
    slice_width = out_weight.shape[1] // lax.axis_size("head")
    partial_sum = jnp.dot(hidden, out_weight, preferred_element_type=jnp.float32)
    mixed = lax.psum_scatter(
        partial_sum.reshape(local_rows, lax.axis_size("head") * 1, slice_width)
        .transpose(1, 0, 2)
        .astype(jnp.bfloat16),
        "head",
        scatter_dimension=0,
        tiled=True,
    ).astype(jnp.float32)
    return (mixed[0].astype(jnp.bfloat16), owned)


def solution(mesh):
    return jax.shard_map(
        body,
        mesh=mesh,
        in_specs=(
            P("seq", "head"),
            P("seq", "head"),
            P("seq", "head"),
            P("head", "seq"),
            P("head", "seq"),
            P(),
            P(),
            P(),
            P("head", None),
        ),
        out_specs=(P("seq", "head"), P("seq", "head", None, None)),
        check_vma=False,
    )
```

profile of v0, /device:TPU:0, one launch (start us, length us, event | category | flops | bytes accessed | tf_op | source)
XLA Modules:
  0.0 744.7 jit_solution(7089236692102941305)
XLA Ops:
  17.6 4.8 fusion.38
  22.4 316.0 %custom-call.4 = f32[8,8,1,64,64]{3,4,2,1,0:T(8,128)} custom-call(f32[8,8,1,64,64]{4,3,2,1,0:T(8,128)} %fusion.38), custom_call_target="InvertDiagBlocksLowerTriangular" | custom-call | tf_op jit(solution)/shard_map/vmap(jit(_solve_triangular))/vmap()/triangular_solve | solution.py:41
  338.3 4.8 multiply_multiply_fusion
  343.2 3.8 fusion.23
  351.8 134.3 %while.28 = (s32[]{:T(128)}, f32[8,128,128]{2,1,0:T(8,128)S(1)}, f32[8,128,128]{2,1,0:T(8,128)S(1)}, f32[8,8,128,128]{2,3,0,1:T(8,128)}, f32[8,8,128,128]{3,2,0,...) while((s32[]{:T(128)}, f32[8,128,128]{2,1,0:T(8,128)S(1)}, ...), condition=%wide.region_6.7_spmd.clone, body=%wide.region_5.6_spmd.clone.sunk | while | flops 404422656 | bytes 9705740 | solution.py:135
  360.2 2.6 convolution_add_fusion.5
  366.3 2.6 convolution_subtract_fusion.5
  376.9 2.6 convolution_add_fusion.5
  383.0 2.6 convolution_subtract_fusion.5
  393.7 2.6 convolution_add_fusion.5
  399.7 2.6 convolution_subtract_fusion.5
  410.4 2.6 convolution_add_fusion.5
  416.4 2.6 convolution_subtract_fusion.5
  427.1 2.6 convolution_add_fusion.5
  433.2 2.6 convolution_subtract_fusion.5
  443.9 2.6 convolution_add_fusion.5
  449.9 2.6 convolution_subtract_fusion.5
  460.6 2.6 convolution_add_fusion.5
  466.7 2.6 convolution_subtract_fusion.5
  477.4 2.6 convolution_add_fusion.5
  483.5 2.6 convolution_subtract_fusion.5
  487.0 114.4 %while.27 = (s32[]{:T(128)}, f32[8,128,128]{2,1,0:T(8,128)}, f32[8,128,128]{2,1,0:T(8,128)S(1)}, f32[8,128,128]{2,1,0:T(8,128)S(1)}, s32[]{:T(128)}) while((s32[]{:T(128)}, f32[8,128,128]{2,1,0:T(8,128)}, f32[8,128,128]{2,1,0:T(8,128)S(1)}, f32[8,128,128]{2,1,0:T(8,128)S(1)}, s32[]{:T(128)}) %tuple.54), condition=%wide.region_8.9_spmd, body=%wide.region_7.8_spmd.sunk | while | flops 201457664 | bytes 4194405 | solution.py:143
  489.4 5.7 collective-permute-start
  495.1 10.7 %collective-permute-done = f32[8,128,128]{2,1,0:T(8,128)} collective-permute-done((f32[8,128,128]{2,1,0:T(8,128)}, f32[8,128,128]{2,1,0:T(8,128)}, u32[]{:S(2)}, u32[]{:S(2)}) %collective-permute-start) | collective-permute-done | bytes 524320 | tf_op jit(solution)/shard_map/while/body/eval_jaxpr/ppermute | solution.py:19
  508.3 5.2 collective-permute-start
  513.5 9.8 %collective-permute-done = f32[8,128,128]{2,1,0:T(8,128)} collective-permute-done((f32[8,128,128]{2,1,0:T(8,128)}, f32[8,128,128]{2,1,0:T(8,128)}, u32[]{:S(2)}, u32[]{:S(2)}) %collective-permute-start) | collective-permute-done | bytes 524320 | tf_op jit(solution)/shard_map/while/body/eval_jaxpr/ppermute | solution.py:19
  525.7 5.2 collective-permute-start
  530.9 8.9 %collective-permute-done = f32[8,128,128]{2,1,0:T(8,128)} collective-permute-done((f32[8,128,128]{2,1,0:T(8,128)}, f32[8,128,128]{2,1,0:T(8,128)}, u32[]{:S(2)}, u32[]{:S(2)}) %collective-permute-start) | collective-permute-done | bytes 524320 | tf_op jit(solution)/shard_map/while/body/eval_jaxpr/ppermute | solution.py:19
  542.3 6.0 collective-permute-start
  548.3 8.0 %collective-permute-done = f32[8,128,128]{2,1,0:T(8,128)} collective-permute-done((f32[8,128,128]{2,1,0:T(8,128)}, f32[8,128,128]{2,1,0:T(8,128)}, u32[]{:S(2)}, u32[]{:S(2)}) %collective-permute-start) | collective-permute-done | bytes 524320 | tf_op jit(solution)/shard_map/while/body/eval_jaxpr/ppermute | solution.py:19
  558.7 6.1 collective-permute-start
  564.8 7.0 collective-permute-done
  574.3 6.1 collective-permute-start
  580.4 6.2 collective-permute-done
  589.1 6.1 collective-permute-start
  595.2 6.2 collective-permute-done
  601.4 8.2 %bitcast_add_fusion = f32[8,8,128,128]{2,3,0,1:T(8,128)S(1)} fusion(f32[8,8,128,128]{2,3,0,1:T(8,128)} %get-tuple-element.79, f32[8,8,128,128]{3,2,0,1:T(8,128)} %get-tuple-element.83, f32[8,128,128]{2,1,0:T(8,128)} %get-tuple-element.82), kind=kOutput, calls=%fused_computation.40 | convolution fusion | flops 1611661312 | bytes 13107200 | tf_op jit(solution)/shard_map/nhde,hef->nhdf/dot_general | solution.py:144
  609.6 8.3 %fusion.52 = f32[8,8,64,128]{3,2,1,0:T(8,128)S(1)} fusion(f32[8,8,128,128]{2,3,0,1:T(8,128)S(1)} %bitcast_add_fusion, f32[8,8,64,256]{3,2,1,0:T(8,128)S(1)} %copy-done.3), kind=kOutput, calls=%fused_computation.70 | convolution fusion | flops 805830656 | bytes 10485760 | tf_op jit(solution)/shard_map/nhcd,nhde->nhce/dot_general | solution.py:145
  619.3 9.5 %multiply_add_fusion = f32[8,8,128,128]{2,3,0,1:T(8,128)} fusion(f32[8,8,128,128]{2,3,0,1:T(8,128)S(1)} %bitcast_add_fusion, f32[8,8,64,128]{3,2,1,0:T(8,128)S(1)} %fusion.52, f32[8,8,64,128]{3,2,1,0:T(8,128)S(1)} %copy-done.4, f32[8,8]{0,1:T(8,128)S(1)} %copy.70), kind=kOutput, calls=%fused_computation.41 | convolution fusion | flops 807403520 | bytes 12583168 | tf_op jit(solution)/shard_map/nhcd,nhce->nhde/dot_general | solution.py:149
  628.7 5.0 gather_fusion
  633.7 5.1 fusion.28
  638.8 8.7 %all-to-all-start = ((f32[8,1,8,128,128]{3,4,2,1,0:T(8,128)}), f32[8,1,8,128,128]{3,4,2,1,0:T(8,128)}, u32[]{:S(2)}, u32[]{:S(2)}) async-start(f32[8,1,8,128,128]{3,4,2,1,0:T(8,128)} %fusion.28), calls=%async_computation.1 | async-start | bytes 8388608 | tf_op jit(solution)/shard_map/all_to_all | solution.py:153
  652.3 3.4 fusion.70
  655.7 8.1 %fusion.31 = f32[8,8,64,128]{3,2,1,0:T(8,128)S(1)} fusion(f32[8,8,128,128]{2,3,0,1:T(8,128)S(1)} %copy-done.1, f32[8,8,64,128]{3,2,1,0:T(8,128)S(1)} %bitcast.127, f32[8,8,64]{2,1,0:T(8,128)S(1)} %get-tuple-element.156), kind=kOutput, calls=%fused_computation.44 | convolution fusion | flops 805830656 | bytes 8404992 | tf_op jit(solution)/shard_map/nhcd,nhde->nhce/dot_general | solution.py:146
  663.8 3.4 multiply_reduce_fusion
  669.1 6.4 copy.86
  675.5 5.9 convert_bitcast_fusion.1
  681.5 52.7 %all-to-all-done = f32[8,1,8,128,128]{3,4,2,1,0:T(8,128)} async-done(((f32[8,1,8,128,128]{3,4,2,1,0:T(8,128)}), f32[8,1,8,128,128]{3,4,2,1,0:T(8,128)}, u32[]{:S(2)}, u32[]{:S(2)}) %all-to-all-start) | async-done | bytes 4194336 | tf_op jit(solution)/shard_map/all_to_all | solution.py:153
  (152 shorter events, 136.9 us)
Async XLA Ops:
  12.1 1.8 copy-start.11
  15.5 1.9 copy-start.8
  338.3 4.8 copy-start.9
  347.0 1.9 copy-start.2
  348.9 2.6 copy-start.12
  489.4 16.3 %collective-permute-start = (f32[8,128,128]{2,1,0:T(8,128)}, f32[8,128,128]{2,1,0:T(8,128)}, u32[]{:S(2)}, u32[]{:S(2)}) collective-permute-start(f32[8,128,128]{2,1,0:T(8,128)} %convolution_add_fusion.4), channel_id=1, source_target_pairs={{0,4},{4,8},{8,12},{12,16},{16,20},{20,24},{24,28},{1,5},{5,9},{9,... | collective-permute-start | bytes 1572872 | tf_op jit(solution)/shard_map/while/body/eval_jaxpr/ppermute | solution.py:19
  508.3 15.0 %collective-permute-start = (f32[8,128,128]{2,1,0:T(8,128)}, f32[8,128,128]{2,1,0:T(8,128)}, u32[]{:S(2)}, u32[]{:S(2)}) collective-permute-start(f32[8,128,128]{2,1,0:T(8,128)} %convolution_add_fusion.4), channel_id=1, source_target_pairs={{0,4},{4,8},{8,12},{12,16},{16,20},{20,24},{24,28},{1,5},{5,9},{9,... | collective-permute-start | bytes 1572872 | tf_op jit(solution)/shard_map/while/body/eval_jaxpr/ppermute | solution.py:19
  525.7 14.1 %collective-permute-start = (f32[8,128,128]{2,1,0:T(8,128)}, f32[8,128,128]{2,1,0:T(8,128)}, u32[]{:S(2)}, u32[]{:S(2)}) collective-permute-start(f32[8,128,128]{2,1,0:T(8,128)} %convolution_add_fusion.4), channel_id=1, source_target_pairs={{0,4},{4,8},{8,12},{12,16},{16,20},{20,24},{24,28},{1,5},{5,9},{9,... | collective-permute-start | bytes 1572872 | tf_op jit(solution)/shard_map/while/body/eval_jaxpr/ppermute | solution.py:19
  542.3 14.0 %collective-permute-start = (f32[8,128,128]{2,1,0:T(8,128)}, f32[8,128,128]{2,1,0:T(8,128)}, u32[]{:S(2)}, u32[]{:S(2)}) collective-permute-start(f32[8,128,128]{2,1,0:T(8,128)} %convolution_add_fusion.4), channel_id=1, source_target_pairs={{0,4},{4,8},{8,12},{12,16},{16,20},{20,24},{24,28},{1,5},{5,9},{9,... | collective-permute-start | bytes 1572872 | tf_op jit(solution)/shard_map/while/body/eval_jaxpr/ppermute | solution.py:19
  558.7 13.1 %collective-permute-start = (f32[8,128,128]{2,1,0:T(8,128)}, f32[8,128,128]{2,1,0:T(8,128)}, u32[]{:S(2)}, u32[]{:S(2)}) collective-permute-start(f32[8,128,128]{2,1,0:T(8,128)} %convolution_add_fusion.4), channel_id=1, source_target_pairs={{0,4},{4,8},{8,12},{12,16},{16,20},{20,24},{24,28},{1,5},{5,9},{9,... | collective-permute-start | bytes 1572872 | tf_op jit(solution)/shard_map/while/body/eval_jaxpr/ppermute | solution.py:19
  574.3 12.3 %collective-permute-start = (f32[8,128,128]{2,1,0:T(8,128)}, f32[8,128,128]{2,1,0:T(8,128)}, u32[]{:S(2)}, u32[]{:S(2)}) collective-permute-start(f32[8,128,128]{2,1,0:T(8,128)} %convolution_add_fusion.4), channel_id=1, source_target_pairs={{0,4},{4,8},{8,12},{12,16},{16,20},{20,24},{24,28},{1,5},{5,9},{9,... | collective-permute-start | bytes 1572872 | tf_op jit(solution)/shard_map/while/body/eval_jaxpr/ppermute | solution.py:19
  589.1 12.3 %collective-permute-start = (f32[8,128,128]{2,1,0:T(8,128)}, f32[8,128,128]{2,1,0:T(8,128)}, u32[]{:S(2)}, u32[]{:S(2)}) collective-permute-start(f32[8,128,128]{2,1,0:T(8,128)} %convolution_add_fusion.4), channel_id=1, source_target_pairs={{0,4},{4,8},{8,12},{12,16},{16,20},{20,24},{24,28},{1,5},{5,9},{9,... | collective-permute-start | bytes 1572872 | tf_op jit(solution)/shard_map/while/body/eval_jaxpr/ppermute | solution.py:19
  601.4 8.2 %copy-start.3 = (f32[8,8,64,256]{3,2,1,0:T(8,128)S(1)}, f32[8,8,64,256]{3,2,1,0:T(8,128)}, u32[]{:S(2)}) copy-start(f32[8,8,64,256]{3,2,1,0:T(8,128)} %copy-done.2) | copy-start | bytes 12582916
  609.6 8.5 %copy-start = (f32[8,8,128,128]{2,3,0,1:T(8,128)}, f32[8,8,128,128]{2,3,0,1:T(8,128)S(1)}, u32[]{:S(2)}) copy-start(f32[8,8,128,128]{2,3,0,1:T(8,128)S(1)} %bitcast_add_fusion) | copy-start | bytes 12582916
  609.6 8.3 %copy-start.13 = (s32[4]{0:T(128)S(1)}, s32[4]{0:T(128)}, u32[]{:S(2)}) copy-start(s32[4]{0:T(128)} %param.19) | copy-start | bytes 52
  609.6 9.6 %copy-start.4 = (f32[8,8,64,128]{3,2,1,0:T(8,128)S(1)}, f32[8,8,64,128]{3,2,1,0:T(8,128)}, u32[]{:S(2)}) copy-start(f32[8,8,64,128]{3,2,1,0:T(8,128)} %get-tuple-element.306) | copy-start | bytes 6291460
  617.9 1.3 copy-start.5
  638.8 8.8 %copy-start.10 = (bf16[512,512]{1,0:T(8,128)(2,1)S(1)}, bf16[512,512]{1,0:T(8,128)(2,1)}, u32[]{:S(2)}) copy-start(bf16[512,512]{1,0:T(8,128)(2,1)} %param.13) | copy-start | bytes 1572868
  638.8 95.4 %all-to-all-start = ((f32[8,1,8,128,128]{3,4,2,1,0:T(8,128)}), f32[8,1,8,128,128]{3,4,2,1,0:T(8,128)}, u32[]{:S(2)}, u32[]{:S(2)}) async-start(f32[8,1,8,128,128]{3,4,2,1,0:T(8,128)} %fusion.28), calls=%async_computation.1 | async-start | bytes 8388608 | tf_op jit(solution)/shard_map/all_to_all | solution.py:153
  647.5 90.1 %reduce-scatter.2.cloned.1.call-start = ((), (), s32[]{:S(2)}) async-start(), calls=%async_computation.2 | async-start | bytes 2621440 | tf_op jit(solution)/shard_map/reduce_scatter | solution.py:158
  648.9 2.0 copy-start.7
  652.3 3.4 copy-start.1
  655.7 8.1 %copy-start.6 = (f32[8,8,64,128]{3,2,1,0:T(8,128)S(1)}, f32[8,8,64,128]{3,2,1,0:T(8,128)}, u32[]{:S(2)}) copy-start(f32[8,8,64,128]{3,2,1,0:T(8,128)} %copy-done.5) | copy-start | bytes 6291460
  663.8 3.4 copy-start.14
Sparse Core Ops, SparseCore 0:
  681.6 32.7 reduce-scatter.1
where the time goes:
time: 754 us; the launch traced here: 745 us
  other arithmetic  359 us (48%)
  matrix products  148 us (20%)
  waiting for transfers between devices  109 us (14%)
  local copies, waits for them, and re-layouts  63.5 us (8%)
  starting transfers between devices  49.1 us (7%)
  between operations  14.7 us (2%)
    another operation x2, other arithmetic, stretch_terms(): jax.scipy.linalg.solve_triangular(system, targets, lower=True, unit_diago...  316 us
    ppermute x7, waiting for transfers between devices, passed_along(): return lax.ppermute(block, axis, route)  56.7 us
    all_to_all x1, waiting for transfers between devices, body(): lax.all_to_all(outbound[:, None], 'seq', split_axis=0, concat_axis=1, til...  52.7 us
    ppermute x7, starting transfers between devices, passed_along(): return lax.ppermute(block, axis, route)  40.4 us
    dynamic_update_slice x16, local copies, waits for them, and re-layouts, body(): lax.scan(walk, (empty_state, identity), (key_mix, fresh_base, retain, key...  31.4 us
    dot_general x8, matrix products, walk(): jnp.einsum('hcd,hce->hde', decay_rows, pulled, precision=HIGH)  20.8 us
    dot_general x8, matrix products, walk(): jnp.einsum('hcd,hce->hde', decay_rows, fresh, precision=HIGH)  20.6 us
    dot_general x8, matrix products, walk(): jnp.einsum('hcd,hde->hce', mix_rows, state, precision=HIGH)  17.4 us
  transfers between devices with their start and end apart: 9, of which 8 were waited for; matrix products, arithmetic and copies ran while one was open for 5% of the time, Pallas kernels for 0%

commit v1 on v0

v1 whole, which is shorter than its diff:
```python
import functools

import jax
import jax.numpy as jnp
from jax import lax
from jax.experimental import pallas as pl
from jax.experimental.pallas import tpu as pltpu
from jax.sharding import PartitionSpec as P

DK = 128
DV = 128
STRETCH = 64
PAIR = 2 * STRETCH
BF = jnp.bfloat16
F32 = jnp.float32
HIGH = lax.Precision.HIGHEST


def mm(a, b):
    return jnp.dot(a, b, preferred_element_type=F32)


def mm_t(a, b):
    return lax.dot_general(a, b, (((1,), (1,)), ((), ())), preferred_element_type=F32)


def split(x):
    high = x.astype(BF)
    return high, (x - high.astype(F32)).astype(BF)


def local_kernel(
    repeat, prompts, ps_ref, q_ref, k_ref, v_ref, gate_ref, rate_ref,
    o_ref, y_ref, l_ref, m_ref, cl_ref, cm_ref,
):
    h = pl.program_id(0)
    rows = q_ref.shape[0]
    number = rows // STRETCH
    blocks = rows // PAIR
    base = lax.axis_index("seq") * number
    ri = lax.broadcasted_iota(jnp.int32, (PAIR, PAIR), 0)
    ci = lax.broadcasted_iota(jnp.int32, (PAIR, PAIR), 1)
    same = (ri // STRETCH) == (ci // STRETCH)
    eye = ri == ci
    strict_mask = same & (ri > ci)
    causal_mask = same & (ri >= ci)
    eye_f = eye.astype(F32)
    eye_b = eye_f.astype(BF)
    upto = (same & (ri <= ci)).astype(F32)
    after = (same & (ri > ci)).astype(F32)
    first_half = lax.broadcasted_iota(jnp.int32, (PAIR, 1), 0) < STRETCH

    gram, scores0, keys, keys_t, qs, qscale = [], [], [], [], [], []
    rk_row, rk_col = [], []
    for c in range(blocks):
        sl = slice(c * PAIR, (c + 1) * PAIR)
        k = k_ref[sl, :]
        q = q_ref[sl, :]
        g = mm_t(k, k)
        s = mm_t(q, k)
        gram.append(g)
        scores0.append(s)
        keys.append(k)
        keys_t.append(k.T)
        diag = jnp.where(eye, g, 0.0)
        rk_row.append(lax.rsqrt(jnp.sum(diag, axis=0, keepdims=True) + 1e-06))
        rk_col.append(lax.rsqrt(jnp.sum(diag, axis=1, keepdims=True) + 1e-06))
        qf = q.astype(F32)
        qs.append(qf)
        qscale.append(lax.rsqrt(jnp.sum(qf * qf, axis=1, keepdims=True) + 1e-06) * DK ** (-0.5))

    grow_all, suf_all = [], []
    for c in range(blocks):
        gate = gate_ref[:, c * PAIR:(c + 1) * PAIR]
        grow_all.append(jnp.dot(gate, upto, preferred_element_type=F32, precision=HIGH))
        suf_all.append(jnp.dot(gate, after, preferred_element_type=F32, precision=HIGH))
    head_row = lax.broadcasted_iota(jnp.int32, (gate_ref.shape[0], PAIR), 0)
    items = [(c, r) for r in range(repeat) for c in range(blocks)]
    lower, inv, info = [], [], []
    for c, r in items:
        sl = slice(c * PAIR, (c + 1) * PAIR)
        pick = head_row == h * repeat + r
        grow, suf, rate = [
            jnp.sum(jnp.where(pick, x, 0.0), axis=0, keepdims=True)
            for x in (grow_all[c], suf_all[c], rate_ref[:, sl])
        ]
        stack = jnp.concatenate([grow, suf, rate, jnp.zeros((5, PAIR), F32)], axis=0)
        cols = stack.T
        gcol, sufcol, bcol = cols[:, 0:1], cols[:, 1:2], cols[:, 2:3]
        decay = jnp.exp(jnp.where(causal_mask, gcol - grow, -jnp.inf))
        a = jnp.where(strict_mask, (bcol * rk_col[c]) * gram[c] * rk_row[c] * decay, 0.0)
        sc = scores0[c] * (qscale[c] * rk_row[c]) * decay
        lower.append(a)
        inv.append(jnp.where(eye, 1.0, jnp.where((ri // 2) == (ci // 2), -a, 0.0)))
        info.append((grow, rate, gcol, sufcol, sc))

    size = 2
    while size < STRETCH:
        off = ((ri // (2 * size)) == (ci // (2 * size))) & ((ri // size) != (ci // size))
        invb = [t.astype(BF) for t in inv]
        part = [
            mm(jnp.where(off, a, 0.0).astype(BF), tb).astype(BF) for a, tb in zip(lower, invb)
        ]
        inv = [t - mm(tb, p) for t, tb, p in zip(inv, invb, part)]
        size *= 2

    solved = []
    invb = [t.astype(BF) for t in inv]
    resid = []
    for a, tb in zip(lower, invb):
        hi, lo = split(a)
        resid.append((eye_f - tb.astype(F32)) - (mm(hi, tb) + mm(lo, tb)))
    inv = [tb.astype(F32) + mm(tb, e.astype(BF)) for tb, e in zip(invb, resid)]
    wu = []
    for (c, r), t, (grow, rate, gcol, sufcol, sc) in zip(items, inv, info):
        sl = slice(c * PAIR, (c + 1) * PAIR)
        v = v_ref[sl, r * DV:(r + 1) * DV]
        wh, wl = split(t * (rate * jnp.exp(grow) * rk_row[c]))
        uh, ul = split(t * rate)
        w = mm(wh, keys[c]) + mm(wl, keys[c])
        u = mm(uh, v) + mm(ul, v)
        wu.append((w, u))
    trans, qside = [], []
    for (c, r), (w, u), (grow, rate, gcol, sufcol, sc) in zip(items, wu, info):
        both = jnp.concatenate([w, u], axis=1)
        d = jnp.exp(sufcol) * rk_col[c]
        scaled = both * d
        t0 = mm(keys_t[c], jnp.where(first_half, scaled, 0.0).astype(BF))
        t1 = mm(keys_t[c], jnp.where(first_half, 0.0, scaled).astype(BF))
        sw = mm(sc.astype(BF), both.astype(BF))
        qe = qs[c] * (qscale[c] * jnp.exp(gcol)) - sw[:, :DK]
        trans.append((t0, t1))
        qside.append((qe.astype(BF), sw[:, DK:]))

    finish = []
    begin = []
    total = jnp.int32(0)
    for p in range(prompts):
        begin.append(total)
        total = total + ps_ref[p]
        finish.append(total)

    cl_ref[...] = jnp.zeros_like(cl_ref)
    cm_ref[...] = jnp.zeros_like(cm_ref)
    zero = jnp.zeros((DK, DV), F32)
    states = [jnp.concatenate([zero, eye_f], axis=1) for _ in range(repeat)]
    for n in range(number):
        c, half = n // 2, n % 2
        opens = begin[0] == base + n
        for p in range(1, prompts):
            opens = opens | (begin[p] == base + n)
        closing = jnp.int32(-1)
        for p in range(prompts):
            closing = jnp.where(finish[p] == base + n + 1, jnp.int32(p), closing)
        keep = jnp.where(opens, 0.0, 1.0).astype(F32)
        following = []
        for r in range(repeat):
            i = r * blocks + c
            x = states[r] * keep
            xb = x.astype(BF)
            hs = slice(half * STRETCH, (half + 1) * STRETCH)
            rs = slice(n * STRETCH, (n + 1) * STRETCH)
            qe, su = qside[i]
            oy = mm(qe[hs], xb)
            cs = slice(r * DV, (r + 1) * DV)
            o_ref[rs, cs] = oy[:, :DV] + su[hs]
            y_ref[rs, cs] = oy[:, DV:].astype(BF)
            t = trans[i][half]
            last = (half + 1) * STRETCH - 1
            retain = jnp.exp(info[i][0][:, last:last + 1])
            moved = retain * x - mm(t[:, :DK].astype(BF), xb)
            following.append(
                jnp.concatenate([moved[:, :DV] + t[:, DK:], moved[:, DV:]], axis=1)
            )
        states = following

        @pl.when(closing >= 0)
        def _(following=following, closing=closing):
            for r in range(repeat):
                cl_ref[closing, r] = following[r][:, :DV]
                cm_ref[closing, r] = following[r][:, DV:].astype(BF)

    for r in range(repeat):
        l_ref[r] = states[r][:, :DV]
        m_ref[r] = states[r][:, DV:].astype(BF)


def local_part(queries, key_vectors, values, gate_log, write_rate, prompt_stretches):
    rows = queries.shape[0]
    heads = gate_log.shape[0]
    groups = queries.shape[1] // DK
    repeat = heads // groups
    prompts = prompt_stretches.shape[0]
    whole = pl.BlockSpec((heads, rows), lambda h: (0, 0))
    wide = pl.BlockSpec((rows, repeat * DV), lambda h: (0, h))
    return pl.pallas_call(
        functools.partial(local_kernel, repeat, prompts),
        grid=(groups,),
        in_specs=[
            pl.BlockSpec(memory_space=pltpu.SMEM),
            pl.BlockSpec((rows, DK), lambda h: (0, h)),
            pl.BlockSpec((rows, DK), lambda h: (0, h)),
            wide,
            whole,
            whole,
        ],
        out_specs=[
            wide,
            wide,
            pl.BlockSpec((repeat, DK, DV), lambda h: (h, 0, 0)),
            pl.BlockSpec((repeat, DK, DK), lambda h: (h, 0, 0)),
            pl.BlockSpec((prompts, repeat, DK, DV), lambda h: (0, h, 0, 0)),
            pl.BlockSpec((prompts, repeat, DK, DK), lambda h: (0, h, 0, 0)),
        ],
        out_shape=[
            jax.ShapeDtypeStruct((rows, heads * DV), F32),
            jax.ShapeDtypeStruct((rows, heads * DV), BF),
            jax.ShapeDtypeStruct((heads, DK, DV), F32),
            jax.ShapeDtypeStruct((heads, DK, DK), BF),
            jax.ShapeDtypeStruct((prompts, heads, DK, DV), F32),
            jax.ShapeDtypeStruct((prompts, heads, DK, DK), BF),
        ],
        compiler_params=pltpu.CompilerParams(vmem_limit_bytes=48 * 1024 * 1024),
    )(prompt_stretches, queries, key_vectors, values, gate_log, write_rate)


def finish_kernel(heads, o_ref, y_ref, inc_ref, cl_ref, cm_ref, gain_ref, w_ref, part_ref, table_ref, hid):
    step = pl.program_id(0)

    @pl.when(step == 0)
    def _():
        gain = gain_ref[...]
        for j in range(heads):
            cs = slice(j * DV, (j + 1) * DV)
            out = o_ref[:, cs] + mm(y_ref[:, cs], inc_ref[j])
            mean = jnp.mean(out * out, axis=1, keepdims=True)
            hid[:, cs] = (out * lax.rsqrt(mean + 1e-06) * gain).astype(BF)

    for j in range(heads):
        table_ref[0, j] = (cl_ref[0, j] + mm(cm_ref[0, j], inc_ref[j])).astype(BF)
    part_ref[0] = mm(hid[...], w_ref[...]).astype(BF)


def finish_part(o_loc, y_map, incoming, close_l, close_m, norm_gain, out_weight, parts):
    rows, width = o_loc.shape
    heads = width // DV
    prompts = close_l.shape[0]
    assert prompts <= parts
    cols = out_weight.shape[1] // parts
    full = pl.BlockSpec((rows, width), lambda s: (0, 0))
    return pl.pallas_call(
        functools.partial(finish_kernel, heads),
        grid=(parts,),
        in_specs=[
            full,
            full,
            pl.BlockSpec((heads, DK, DV), lambda s: (0, 0, 0)),
            pl.BlockSpec((1, heads, DK, DV), lambda s: (jnp.minimum(s, prompts - 1), 0, 0, 0)),
            pl.BlockSpec((1, heads, DK, DK), lambda s: (jnp.minimum(s, prompts - 1), 0, 0, 0)),
            pl.BlockSpec((1, DV), lambda s: (0, 0)),
            pl.BlockSpec((width, cols), lambda s: (0, s)),
        ],
        out_specs=[
            pl.BlockSpec((1, rows, cols), lambda s: (s, 0, 0)),
            pl.BlockSpec((1, heads, DK, DV), lambda s: (jnp.minimum(s, prompts - 1), 0, 0, 0)),
        ],
        out_shape=[
            jax.ShapeDtypeStruct((parts, rows, cols), BF),
            jax.ShapeDtypeStruct((prompts, heads, DK, DV), BF),
        ],
        scratch_shapes=[pltpu.VMEM((rows, width), BF)],
        compiler_params=pltpu.CompilerParams(vmem_limit_bytes=48 * 1024 * 1024),
    )(o_loc, y_map, incoming, close_l, close_m, norm_gain.reshape(1, -1), out_weight)


def relay(local_state, local_map, devices_seq):
    route = [(i, i + 1) for i in range(devices_seq - 1)]
    incoming = lax.ppermute(local_state.astype(BF), "seq", route)
    for _ in range(devices_seq // 2 - 1):
        outgoing = jnp.einsum("hde,hef->hdf", local_map, incoming, preferred_element_type=F32)
        incoming = lax.ppermute((outgoing + local_state).astype(BF), "seq", route)
    return incoming


def body(
    queries, key_vectors, values, gate_log, write_rate,
    prompt_stretches, decode_owner, norm_gain, out_weight,
):
    position = lax.axis_index("seq")
    devices_seq = lax.axis_size("seq")
    o_loc, y_map, local_state, local_map, close_l, close_m = local_part(
        queries, key_vectors, values, gate_log, write_rate, prompt_stretches
    )
    incoming = relay(local_state, local_map, devices_seq)
    parts = lax.axis_size("head")
    partial_sum, table = finish_part(
        o_loc, y_map, incoming, close_l, close_m, norm_gain, out_weight, parts
    )
    table = lax.psum(table, "seq")
    mine = (decode_owner == position).astype(F32)
    owned = jnp.sum(table.astype(F32) * mine[:, None, None, None], axis=0)
    mixed = lax.psum_scatter(partial_sum, "head", scatter_dimension=0, tiled=True)
    return (mixed[0], owned[None])


def solution(mesh):
    return jax.shard_map(
        body,
        mesh=mesh,
        in_specs=(
            P("seq", "head"),
            P("seq", "head"),
            P("seq", "head"),
            P("head", "seq"),
            P("head", "seq"),
            P(),
            P(),
            P(),
            P("head", None),
        ),
        out_specs=(P("seq", "head"), P("seq", "head", None, None)),
        check_vma=False,
    )
```

time: 754 us -> 175 us (0.23); the launches traced: 745 us -> 174 us
  other arithmetic: 359 us -> 2.38 us
  matrix products: 148 us -> 0.65 us
  local copies, waits for them, and re-layouts: 63.5 us -> 5.44 us
  Pallas kernels: 0 us -> 31.3 us
  starting transfers between devices: 49.1 us -> 19 us
  waiting for transfers between devices: 109 us -> 100 us
    another operation x6 -> x0, other arithmetic: 318 us -> none  [the longest x2 316 us: stretch_terms(): jax.scipy.linalg.solve_triangular(system, targets, lower=True, unit_diago...]
    dot_general x47 -> x3, matrix products: 144 us -> 0.65 us  [relay(): jnp.einsum('hde,hef->hdf', local_map, incoming, preferred_element_type=F32)]
    psum x0 -> x1, waiting for transfers between devices: none -> 81.5 us  [body(): table = lax.psum(table, 'seq')]
    all_to_all x1 -> x0, waiting for transfers between devices: 52.7 us -> none  [body(): lax.all_to_all(outbound[:, None], 'seq', split_axis=0, concat_axis=1, til...]
    ppermute x7 -> x4, waiting for transfers between devices: 56.7 us -> 17.9 us  [the longest x3 12.4 us: relay(): incoming = lax.ppermute((outgoing + local_state).astype(BF), 'seq', route)]
    dynamic_update_slice x16 -> x0, local copies, waits for them, and re-layouts: 31.4 us -> none  [body(): lax.scan(walk, (empty_state, identity), (key_mix, fresh_base, retain, key...]
    pallas_call x0 -> x2, Pallas kernels: none -> 31.3 us  [the longest x1 23.3 us: local_part(): pl.pallas_call(functools.partial(local_kernel, repeat, prompts), grid=(gr...]
    ppermute x7 -> x4, starting transfers between devices: 40.4 us -> 18.9 us  [the longest x3 14 us: relay(): incoming = lax.ppermute((outgoing + local_state).astype(BF), 'seq', route)]
  transfers between devices with their start and end apart: 9 -> 6, of which waited for: 8 -> 5; matrix products, arithmetic and copies ran while one was open for 5% -> 1% of each run, Pallas kernels for 0% -> 0%
where the time goes in v1:
time: 175 us; the launch traced here: 174 us
  waiting for transfers between devices  100 us (57%)
  Pallas kernels  31.3 us (18%)
  starting transfers between devices  19 us (11%)
  between operations  15.6 us (9%)
  local copies, waits for them, and re-layouts  5.44 us (3%)
  other arithmetic  2.38 us (1%)
    psum x1, waiting for transfers between devices, body(): table = lax.psum(table, 'seq')  81.5 us
    pallas_call x1, Pallas kernels, local_part(): pl.pallas_call(functools.partial(local_kernel, repeat, prompts), grid=(gr...  23.3 us
    ppermute x3, starting transfers between devices, relay(): incoming = lax.ppermute((outgoing + local_state).astype(BF), 'seq', route)  14 us
    ppermute x3, waiting for transfers between devices, relay(): incoming = lax.ppermute((outgoing + local_state).astype(BF), 'seq', route)  12.4 us
    pallas_call x1, Pallas kernels, finish_part(): pl.pallas_call(functools.partial(finish_kernel, heads), grid=(parts,), in...  7.93 us
    ppermute x1, waiting for transfers between devices, relay(): incoming = lax.ppermute(local_state.astype(BF), 'seq', route)  5.53 us
    unnamed x16, local copies, waits for them, and re-layouts  5.44 us
    ppermute x1, starting transfers between devices, relay(): incoming = lax.ppermute(local_state.astype(BF), 'seq', route)  4.93 us
  transfers between devices with their start and end apart: 6, of which 5 were waited for; matrix products, arithmetic and copies ran while one was open for 1% of the time, Pallas kernels for 0%

profile of v1, /device:TPU:0, one launch (start us, length us, event | category | flops | bytes accessed | tf_op | source)
XLA Modules:
  0.0 174.3 jit_solution(4072450617827487542)
XLA Ops:
  8.0 0.0 all-reduce.2.cloned.1.call-start
  8.0 0.0 copy-start
  8.1 1.2 copy-done
  9.3 0.0 copy-start.1
  9.3 1.0 copy-done.1
  10.3 0.0 copy-start.2
  10.3 1.0 copy-done.2
  11.4 0.0 copy-start.3
  11.4 0.7 copy-done.3
  12.1 0.0 copy-start.4
  12.1 0.7 copy-done.4
  12.8 0.0 copy-start.5
  12.8 0.7 copy-done.5
  13.4 23.3 %shard_map.104 = (f32[512,1024]{1,0:T(8,128)}, bf16[512,1024]{1,0:T(8,128)(2,1)S(1)}, f32[8,128,128]{2,1,0:T(8,128)S(1)}, bf16[8,128,128]{2,1,0:T(8,128)(2,1)S(1...) custom-call(s32[4]{0:T(128)S(1)} %copy-done.5, bf16[512,512]{1,0:T(8,128)(2,1)S(1)} %copy-done.1, ...), custom_call_target="tpu_custom_call" | custom-call | tf_op jit(solution)/shard_map/pallas_call | solution.py:196
  36.8 0.0 copy-start.6
  36.8 4.9 %collective-permute-start = (bf16[8,128,128]{2,1,0:T(8,128)(2,1)S(1)}, bf16[8,128,128]{2,1,0:T(8,128)(2,1)S(1)}, u32[]{:S(2)}, u32[]{:S(2)}) collective-permute-start(bf16[8,128,128]{2,1,0:T(8,128)(2,1)S(1)} %convert_element_type.18), channel_id=1, source_target_pairs={{0,4},{4,8},{8,12},{12,16},{16,20},{20,24},{24,28},{1,5},{5,9},{9,... | collective-permute-start | bytes 786440 | tf_op jit(solution)/shard_map/ppermute | solution.py:278
  41.8 5.5 %collective-permute-done = bf16[8,128,128]{2,1,0:T(8,128)(2,1)S(1)} collective-permute-done((bf16[8,128,128]{2,1,0:T(8,128)(2,1)S(1)}, bf16[8,128,128]{2,1,0:T(8,128)(2,1)S(1)}, u32[]{:S(2)}, u32[]{:S(2)}) %collective-permute-start) | collective-permute-done | bytes 262176 | tf_op jit(solution)/shard_map/ppermute | solution.py:278
  47.3 0.2 fusion
  47.5 4.4 %collective-permute-start.1 = (bf16[8,128,128]{2,1,0:T(8,128)(2,1)S(1)}, bf16[8,128,128]{2,1,0:T(8,128)(2,1)S(1)}, u32[]{:S(2)}, u32[]{:S(2)}) collective-permute-start(bf16[8,128,128]{2,1,0:T(8,128)(2,1)S(1)} %fusion), channel_id=1, source_target_pairs={{0,4},{4,8},{8,12},{12,16},{16,20},{20,24},{24,28},{1,5},{5,9},{9,... | collective-permute-start | bytes 786440 | tf_op jit(solution)/shard_map/ppermute | solution.py:281
  51.9 4.7 %collective-permute-done.1 = bf16[8,128,128]{2,1,0:T(8,128)(2,1)S(1)} collective-permute-done((bf16[8,128,128]{2,1,0:T(8,128)(2,1)S(1)}, bf16[8,128,128]{2,1,0:T(8,128)(2,1)S(1)}, u32[]{:S(2)}, u32[]{:S(2)}) %collective-permute-start.1) | collective-permute-done | bytes 262176 | tf_op jit(solution)/shard_map/ppermute | solution.py:281
  56.6 0.2 fusion.1
  56.8 4.4 %collective-permute-start.2 = (bf16[8,128,128]{2,1,0:T(8,128)(2,1)S(1)}, bf16[8,128,128]{2,1,0:T(8,128)(2,1)S(1)}, u32[]{:S(2)}, u32[]{:S(2)}) collective-permute-start(bf16[8,128,128]{2,1,0:T(8,128)(2,1)S(1)} %fusion.1), channel_id=1, source_target_pairs={{0,4},{4,8},{8,12},{12,16},{16,20},{20,24},{24,28},{1,5},{5,9},{9,... | collective-permute-start | bytes 786440 | tf_op jit(solution)/shard_map/ppermute | solution.py:281
  61.2 3.9 %collective-permute-done.2 = bf16[8,128,128]{2,1,0:T(8,128)(2,1)S(1)} collective-permute-done((bf16[8,128,128]{2,1,0:T(8,128)(2,1)S(1)}, bf16[8,128,128]{2,1,0:T(8,128)(2,1)S(1)}, u32[]{:S(2)}, u32[]{:S(2)}) %collective-permute-start.2) | collective-permute-done | bytes 262176 | tf_op jit(solution)/shard_map/ppermute | solution.py:281
  65.1 0.2 fusion.2
  65.3 5.2 %collective-permute-start.3 = (bf16[8,128,128]{2,1,0:T(8,128)(2,1)S(1)}, bf16[8,128,128]{2,1,0:T(8,128)(2,1)S(1)}, u32[]{:S(2)}, u32[]{:S(2)}) collective-permute-start(bf16[8,128,128]{2,1,0:T(8,128)(2,1)S(1)} %fusion.2), channel_id=1, source_target_pairs={{0,4},{4,8},{8,12},{12,16},{16,20},{20,24},{24,28},{1,5},{5,9},{9,... | collective-permute-start | bytes 786440 | tf_op jit(solution)/shard_map/ppermute | solution.py:281
  70.5 3.9 %collective-permute-done.3.inc_ref = bf16[8,128,128]{2,1,0:T(8,128)(2,1)S(1)} collective-permute-done((bf16[8,128,128]{2,1,0:T(8,128)(2,1)S(1)}, bf16[8,128,128]{2,1,0:T(8,128)(2,1)S(1)}, u32[]{:S(2)}, u32[]{:S(2)}) %collective-permute-start.3) | collective-permute-done | bytes 262176 | tf_op jit(solution)/shard_map/ppermute | solution.py:281
  74.4 0.0 copy-done.6
  74.4 7.9 %shard_map.105 = (bf16[4,512,512]{2,1,0:T(8,128)(2,1)}, bf16[4,8,128,128]{3,2,1,0:T(8,128)(2,1)}) custom-call(f32[512,1024]{1,0:T(8,128)} %get-tuple-element.10.o_ref, bf16[512,1024]{1,0:T(8,128)(2,1)S(1)} %get-tuple-element.11.y_ref, bf16[8,128,128]{2,1,0:T(8,128)(2,1)S(1)} %collective-permute-done.3.inc_ref, f32[4,8,128,128]{3,2,1,0:T(8,128)} %get-tuple-element.14.cl_ref, ...), custom_call_target="tpu_custom_call" | custom-call | tf_op jit(solution)/shard_map/pallas_call | solution.py:251
  82.3 0.0 copy-start.7
  82.3 0.0 all-reduce.2.cloned.1.call-update
  82.3 0.0 reduce-scatter.2.cloned.1.call-start
  82.4 0.5 reduce-scatter.2.cloned.1.call-update
  82.9 0.0 copy-done.7
  83.0 81.5 %all-reduce.2.cloned.1.call-done = bf16[4,8,128,128]{3,2,1,0:T(8,128)(2,1)} async-done(((bf16[4,8,128,128]{3,2,1,0:T(8,128)(2,1)}), bf16[4,8,128,128]{3,2,1,0:T(8,128)(2,1)}) %all-reduce.2.cloned.1.call-update) | async-done | bytes 1048592 | tf_op jit(solution)/shard_map/psum | solution.py:299
  164.5 2.3 %multiply_reduce_fusion = f32[8,128,128]{2,1,0:T(8,128)} fusion(bf16[4,8,128,128]{3,2,1,0:T(8,128)(2,1)} %all-reduce.2.cloned.1.call-done, f32[4]{0:T(128)S(1)} %compare_convert_fusion), kind=kLoop, calls=%fused_computation | loop fusion | flops 1441792 | bytes 1572880 | tf_op jit(solution)/shard_map/reduce_sum | solution.py:301
  166.9 0.0 reduce-scatter.2.cloned.1.call-done
  (2 shorter events, 0.0 us)
Async XLA Ops:
  8.0 156.5 %all-reduce.2.cloned.1.call-start = ((), (), s32[]{:S(2)}) async-start(), calls=%async_computation.2 | async-start | bytes 2097152 | tf_op jit(solution)/shard_map/psum | solution.py:299
  8.0 1.2 copy-start
  9.3 1.0 copy-start.1
  10.3 1.0 copy-start.2
  11.4 0.7 copy-start.3
  12.1 0.7 copy-start.4
  12.8 0.7 copy-start.5
  36.8 37.6 %copy-start.6 = (f32[128]{0:T(128)S(1)}, f32[128]{0:T(128)}, u32[]{:S(2)}) copy-start(f32[128]{0:T(128)} %param.16) | copy-start | bytes 1540
  36.8 10.5 %collective-permute-start = (bf16[8,128,128]{2,1,0:T(8,128)(2,1)S(1)}, bf16[8,128,128]{2,1,0:T(8,128)(2,1)S(1)}, u32[]{:S(2)}, u32[]{:S(2)}) collective-permute-start(bf16[8,128,128]{2,1,0:T(8,128)(2,1)S(1)} %convert_element_type.18), channel_id=1, source_target_pairs={{0,4},{4,8},{8,12},{12,16},{16,20},{20,24},{24,28},{1,5},{5,9},{9,... | collective-permute-start | bytes 786440 | tf_op jit(solution)/shard_map/ppermute | solution.py:278
  47.5 9.1 %collective-permute-start.1 = (bf16[8,128,128]{2,1,0:T(8,128)(2,1)S(1)}, bf16[8,128,128]{2,1,0:T(8,128)(2,1)S(1)}, u32[]{:S(2)}, u32[]{:S(2)}) collective-permute-start(bf16[8,128,128]{2,1,0:T(8,128)(2,1)S(1)} %fusion), channel_id=1, source_target_pairs={{0,4},{4,8},{8,12},{12,16},{16,20},{20,24},{24,28},{1,5},{5,9},{9,... | collective-permute-start | bytes 786440 | tf_op jit(solution)/shard_map/ppermute | solution.py:281
  56.8 8.3 %collective-permute-start.2 = (bf16[8,128,128]{2,1,0:T(8,128)(2,1)S(1)}, bf16[8,128,128]{2,1,0:T(8,128)(2,1)S(1)}, u32[]{:S(2)}, u32[]{:S(2)}) collective-permute-start(bf16[8,128,128]{2,1,0:T(8,128)(2,1)S(1)} %fusion.1), channel_id=1, source_target_pairs={{0,4},{4,8},{8,12},{12,16},{16,20},{20,24},{24,28},{1,5},{5,9},{9,... | collective-permute-start | bytes 786440 | tf_op jit(solution)/shard_map/ppermute | solution.py:281
  65.3 9.1 %collective-permute-start.3 = (bf16[8,128,128]{2,1,0:T(8,128)(2,1)S(1)}, bf16[8,128,128]{2,1,0:T(8,128)(2,1)S(1)}, u32[]{:S(2)}, u32[]{:S(2)}) collective-permute-start(bf16[8,128,128]{2,1,0:T(8,128)(2,1)S(1)} %fusion.2), channel_id=1, source_target_pairs={{0,4},{4,8},{8,12},{12,16},{16,20},{20,24},{24,28},{1,5},{5,9},{9,... | collective-permute-start | bytes 786440 | tf_op jit(solution)/shard_map/ppermute | solution.py:281
  82.3 0.7 copy-start.7
  82.3 84.5 %reduce-scatter.2.cloned.1.call-start = ((), (), s32[]{:S(2)}) async-start(), calls=%async_computation.1 | async-start | bytes 2621440 | tf_op jit(solution)/shard_map/reduce_scatter | solution.py:302
Sparse Core Ops, SparseCore 0:
  82.5 82.0 all-reduce.1
Sparse Core Ops, SparseCore 1:
  85.9 35.4 reduce-scatter.1

commit v2 on v1

--- a/solution.py
+++ b/solution.py
@@ -224,62 +224,291 @@
     )(prompt_stretches, queries, key_vectors, values, gate_log, write_rate)
 
 
-def finish_kernel(heads, o_ref, y_ref, inc_ref, cl_ref, cm_ref, gain_ref, w_ref, part_ref, table_ref, hid):
-    step = pl.program_id(0)
-
-    @pl.when(step == 0)
+def tail_kernel(
+    heads, prompts, devices, groups,
+    l_ref, m_ref, mask_ref, gain_ref, o_hbm, y_hbm, cl_hbm, cm_hbm, w_hbm,
+    mixed_ref, owned_ref,
+    o_ref, y_ref, cl_ref, cm_ref, w_ref, inc, nxt, pair_out, pair_in, own,
+    up_in, up_out, down_in, down_out, sel_out, sel_in, hid, core_out, core_in, x_out, x_in,
+    load_sem, chain_s, chain_r, pair_s, pair_r, up_s, up_r, down_s, down_r,
+    sel_s, sel_r, core_s, core_r, x_s, x_r,
+):
+    pos = lax.axis_index("seq")
+    head = lax.axis_index("head")
+    half = prompts // 2
+    xs = groups // 2
+    here, core = head // 2, lax.rem(head, 2)
+    side = lax.rem(pos, 2)
+    mate = pos + 1 - 2 * side
+    right, left = lax.rem(pos + 1, devices), lax.rem(pos + devices - 1, devices)
+    above, below = lax.rem(pos + 2, devices), lax.rem(pos + devices - 2, devices)
+    cols = w_ref.shape[1] // groups
+
+    loads = [
+        pltpu.make_async_copy(src, dst, load_sem.at[i])
+        for i, (src, dst) in enumerate(
+            [(cl_hbm, cl_ref), (cm_hbm, cm_ref), (o_hbm, o_ref), (y_hbm, y_ref), (w_hbm, w_ref)]
+        )
+    ]
+    for load in loads:
+        load.start()
+
+    barrier = pltpu.get_barrier_semaphore()
+    has_left, has_right = pos >= 1, pos <= devices - 2
+    has_below, has_above = pos >= 2, pos <= devices - 3
+    count = jnp.int32(xs)
+    for has, other in (
+        (has_left, left), (has_right, right), (has_below, below), (has_above, above)
+    ):
+        count = count + has.astype(jnp.int32)
+
+        @pl.when(has)
+        def _(other=other):
+            pl.semaphore_signal(
+                barrier, inc=1, device_id={"seq": other}, device_id_type=pl.DeviceIdType.MESH
+            )
+    x_heads = [lax.rem(here + k, xs) * 2 + core for k in range(1, xs)]
+    for other in [here * 2 + 1 - core] + x_heads:
+        pl.semaphore_signal(
+            barrier, inc=1, device_id={"head": other}, device_id_type=pl.DeviceIdType.MESH
+        )
+    pl.semaphore_wait(barrier, count)
+
+    def remote(src, dst, send, recv, **where):
+        return pltpu.make_async_remote_copy(
+            src_ref=src, dst_ref=dst, send_sem=send, recv_sem=recv,
+            device_id=where, device_id_type=pl.DeviceIdType.MESH,
+        )
+
+    def chain(h):
+        return remote(nxt.at[h], inc.at[h], chain_s.at[h], chain_r.at[h], seq=right)
+
+    def pair(h):
+        return remote(pair_out.at[h], pair_in.at[h], pair_s.at[h], pair_r.at[h], seq=mate)
+
+    def upward(h):
+        return remote(up_out.at[h], up_in.at[h], up_s.at[h], up_r.at[h], seq=above)
+
+    def downward(h):
+        return remote(down_out.at[h], down_in.at[h], down_s.at[h], down_r.at[h], seq=below)
+
+    def deliver(h):
+        return remote(sel_out.at[h], sel_in.at[h], sel_s.at[h], sel_r.at[h], seq=mate)
+
+    def to_core(k):
+        return remote(
+            core_out.at[k], core_in.at[k], core_s.at[k], core_r.at[k], head=here * 2 + 1 - core
+        )
+
+    def to_x(k):
+        return remote(
+            x_out.at[k - 1], x_in.at[k - 1], x_s.at[k - 1], x_r.at[k - 1], head=x_heads[k - 1]
+        )
+
+    @pl.when(pos == 0)
     def _():
-        gain = gain_ref[...]
-        for j in range(heads):
-            cs = slice(j * DV, (j + 1) * DV)
-            out = o_ref[:, cs] + mm(y_ref[:, cs], inc_ref[j])
-            mean = jnp.mean(out * out, axis=1, keepdims=True)
-            hid[:, cs] = (out * lax.rsqrt(mean + 1e-06) * gain).astype(BF)
-
+        inc[...] = jnp.zeros_like(inc)
+
+    def chain_step(h, _):
+        @pl.when(has_left)
+        def _():
+            chain(h).wait_recv()
+
+        nxt[h] = (mm(m_ref[h], inc[h]) + l_ref[h]).astype(BF)
+
+        @pl.when(has_right)
+        def _():
+            chain(h).start()
+
+        return 0
+
+    lax.fori_loop(0, heads, chain_step, 0)
+
+    loads[0].wait()
+    loads[1].wait()
+
+    def table(p, h):
+        return (cl_ref[p, h] + mm(cm_ref[p, h], inc[h])).astype(BF)
+
+    def pair_step(h, _):
+        for i in range(half):
+            pair_out[h, i] = table((1 - side) * half + i, h)
+        pair(h).start()
+        for i in range(half):
+            own[h, i] = table(side * half + i, h)
+        return 0
+
+    lax.fori_loop(0, heads, pair_step, 0)
+
+    loads[2].wait()
+    loads[3].wait()
+    gain = gain_ref[...]
     for j in range(heads):
-        table_ref[0, j] = (cl_ref[0, j] + mm(cm_ref[0, j], inc_ref[j])).astype(BF)
-    part_ref[0] = mm(hid[...], w_ref[...]).astype(BF)
-
-
-def finish_part(o_loc, y_map, incoming, close_l, close_m, norm_gain, out_weight, parts):
+        cs = slice(j * DV, (j + 1) * DV)
+        out = o_ref[:, cs] + mm(y_ref[:, cs], inc[j])
+        mean = jnp.mean(out * out, axis=1, keepdims=True)
+        hid[:, cs] = (out * lax.rsqrt(mean + 1e-06) * gain).astype(BF)
+    loads[4].wait()
+
+    def project(k, which):
+        slot = lax.rem(here + k, xs) * 2 + which
+        w = w_ref[:, pl.ds(pl.multiple_of(slot * cols, 128), cols)]
+        return mm(hid[...], w)
+
+    order = list(range(1, xs)) + [0]
+    for k in order:
+        core_out[k] = project(k, 1 - core).astype(BF)
+        to_core(k).start()
+    for k in range(1, xs):
+        mine = project(k, core)
+        to_core(k).wait_recv()
+        x_out[k - 1] = (mine + core_in[k].astype(F32)).astype(BF)
+        to_x(k).start()
+
+    def gather_step(h, _):
+        pair(h).wait_recv()
+        own[h] = own[h] + pair_in[h]
+        return 0
+
+    lax.fori_loop(0, heads, gather_step, 0)
+
+    @pl.when(pos < 2)
+    def _():
+        up_in[...] = jnp.zeros_like(up_in)
+
+    @pl.when(pos >= devices - 2)
+    def _():
+        down_in[...] = jnp.zeros_like(down_in)
+
+    def up_step(h, _):
+        @pl.when(has_below)
+        def _():
+            upward(h).wait_recv()
+
+        @pl.when(has_above)
+        def _():
+            up_out[h] = up_in[h] + own[h]
+            upward(h).start()
+
+        return 0
+
+    def down_step(h, _):
+        @pl.when(has_above)
+        def _():
+            downward(h).wait_recv()
+
+        @pl.when(has_below)
+        def _():
+            down_out[h] = down_in[h] + own[h]
+            downward(h).start()
+
+        return 0
+
+    low = pos < devices // 2
+
+    @pl.when(low)
+    def _():
+        lax.fori_loop(0, heads, up_step, 0)
+        lax.fori_loop(0, heads, down_step, 0)
+
+    @pl.when(jnp.logical_not(low))
+    def _():
+        lax.fori_loop(0, heads, down_step, 0)
+        lax.fori_loop(0, heads, up_step, 0)
+
+    def select_step(h, _):
+        kept = jnp.zeros((DK, DV), F32)
+        sent = jnp.zeros((DK, DV), F32)
+        for i in range(half):
+            full = (up_in[h, i] + own[h, i] + down_in[h, i]).astype(F32)
+            p = side * half + i
+            kept = kept + full * mask_ref[p]
+            sent = sent + full * mask_ref[prompts + p]
+        sel_out[h] = sent.astype(BF)
+        deliver(h).start()
+        owned_ref[0, h] = kept
+        return 0
+
+    lax.fori_loop(0, heads, select_step, 0)
+
+    mine = project(0, core)
+    to_core(0).wait_recv()
+    total = mine + core_in[0].astype(F32)
+    for k in range(1, xs):
+        to_x(k).wait_recv()
+        total = total + x_in[k - 1].astype(F32)
+    mixed_ref[...] = total.astype(BF)
+
+    def last_step(h, _):
+        deliver(h).wait_recv()
+        owned_ref[0, h] = owned_ref[0, h] + sel_in[h].astype(F32)
+        pair(h).wait_send()
+        deliver(h).wait_send()
+
+        @pl.when(has_right)
+        def _():
+            chain(h).wait_send()
+
+        @pl.when(has_above)
+        def _():
+            upward(h).wait_send()
+
+        @pl.when(has_below)
+        def _():
+            downward(h).wait_send()
+
+        return 0
+
+    lax.fori_loop(0, heads, last_step, 0)
+    for k in range(xs):
+        to_core(k).wait_send()
+    for k in range(1, xs):
+        to_x(k).wait_send()
+
+
+def tail_part(local_state, local_map, masks, norm_gain, o_loc, y_map, close_l, close_m, out_weight):
     rows, width = o_loc.shape
     heads = width // DV
     prompts = close_l.shape[0]
-    assert prompts <= parts
-    cols = out_weight.shape[1] // parts
-    full = pl.BlockSpec((rows, width), lambda s: (0, 0))
+    half = prompts // 2
+    devices = lax.axis_size("seq")
+    groups = lax.axis_size("head")
+    xs = groups // 2
+    cols = out_weight.shape[1] // groups
+    vmem = pl.BlockSpec(memory_space=pltpu.VMEM)
+    anywhere = pl.BlockSpec(memory_space=pl.ANY)
+    dma = pltpu.SemaphoreType.DMA
+    line = pltpu.VMEM((heads, half, DK, DV), BF)
+    state = pltpu.VMEM((heads, DK, DV), BF)
     return pl.pallas_call(
-        functools.partial(finish_kernel, heads),
-        grid=(parts,),
-        in_specs=[
-            full,
-            full,
-            pl.BlockSpec((heads, DK, DV), lambda s: (0, 0, 0)),
-            pl.BlockSpec((1, heads, DK, DV), lambda s: (jnp.minimum(s, prompts - 1), 0, 0, 0)),
-            pl.BlockSpec((1, heads, DK, DK), lambda s: (jnp.minimum(s, prompts - 1), 0, 0, 0)),
-            pl.BlockSpec((1, DV), lambda s: (0, 0)),
-            pl.BlockSpec((width, cols), lambda s: (0, s)),
+        functools.partial(tail_kernel, heads, prompts, devices, groups),
+        in_specs=[vmem] * 4 + [anywhere] * 5,
+        out_specs=[vmem, vmem],
+        out_shape=[
+            jax.ShapeDtypeStruct((rows, cols), BF),
+            jax.ShapeDtypeStruct((1, heads, DK, DV), F32),
         ],
-        out_specs=[
-            pl.BlockSpec((1, rows, cols), lambda s: (s, 0, 0)),
-            pl.BlockSpec((1, heads, DK, DV), lambda s: (jnp.minimum(s, prompts - 1), 0, 0, 0)),
-        ],
-        out_shape=[
-            jax.ShapeDtypeStruct((parts, rows, cols), BF),
-            jax.ShapeDtypeStruct((prompts, heads, DK, DV), BF),
-        ],
-        scratch_shapes=[pltpu.VMEM((rows, width), BF)],
-        compiler_params=pltpu.CompilerParams(vmem_limit_bytes=48 * 1024 * 1024),
-    )(o_loc, y_map, incoming, close_l, close_m, norm_gain.reshape(1, -1), out_weight)
-
-
-def relay(local_state, local_map, devices_seq):
-    route = [(i, i + 1) for i in range(devices_seq - 1)]
-    incoming = lax.ppermute(local_state.astype(BF), "seq", route)
-    for _ in range(devices_seq // 2 - 1):
-        outgoing = jnp.einsum("hde,hef->hdf", local_map, incoming, preferred_element_type=F32)
-        incoming = lax.ppermute((outgoing + local_state).astype(BF), "seq", route)
-    return incoming
+        scratch_shapes=[
+            pltpu.VMEM(o_loc.shape, F32),
+            pltpu.VMEM(y_map.shape, BF),
+            pltpu.VMEM(close_l.shape, F32),
+            pltpu.VMEM(close_m.shape, BF),
+            pltpu.VMEM(out_weight.shape, BF),
+            state, state, line, line, line, line, line, line, line, state, state,
+            pltpu.VMEM((rows, width), BF),
+            pltpu.VMEM((xs, rows, cols), BF),
+            pltpu.VMEM((xs, rows, cols), BF),
+            pltpu.VMEM((xs - 1, rows, cols), BF),
+            pltpu.VMEM((xs - 1, rows, cols), BF),
+            dma((5,)),
+        ] + [dma((heads,))] * 10 + [dma((xs,))] * 2 + [dma((xs - 1,))] * 2,
+        compiler_params=pltpu.CompilerParams(
+            collective_id=0, has_side_effects=True, vmem_limit_bytes=48 * 1024 * 1024
+        ),
+    )(
+        local_state, local_map, masks, norm_gain.reshape(1, -1),
+        o_loc, y_map, close_l, close_m, out_weight,
+    )
 
 
 def body(
@@ -287,20 +516,15 @@
     prompt_stretches, decode_owner, norm_gain, out_weight,
 ):
     position = lax.axis_index("seq")
-    devices_seq = lax.axis_size("seq")
     o_loc, y_map, local_state, local_map, close_l, close_m = local_part(
         queries, key_vectors, values, gate_log, write_rate, prompt_stretches
     )
-    incoming = relay(local_state, local_map, devices_seq)
-    parts = lax.axis_size("head")
-    partial_sum, table = finish_part(
-        o_loc, y_map, incoming, close_l, close_m, norm_gain, out_weight, parts
+    mate = position + 1 - 2 * (position % 2)
+    masks = jnp.concatenate([decode_owner == position, decode_owner == mate]).astype(F32)
+    masks = jnp.broadcast_to(masks[:, None, None], (masks.shape[0], 1, DV))
+    return tail_part(
+        local_state, local_map, masks, norm_gain, o_loc, y_map, close_l, close_m, out_weight
     )
-    table = lax.psum(table, "seq")
-    mine = (decode_owner == position).astype(F32)
-    owned = jnp.sum(table.astype(F32) * mine[:, None, None, None], axis=0)
-    mixed = lax.psum_scatter(partial_sum, "head", scatter_dimension=0, tiled=True)
-    return (mixed[0], owned[None])
 
 
 def solution(mesh):

time: 175 us -> 103 us (0.59)
  the two profiles are of different devices: /device:TPU:0 before, /device:TPU:24 now
where the time goes in v2:
time: 103 us; the launch traced here: 102 us
  Pallas kernels  92.2 us (90%)
  local copies, waits for them, and re-layouts  8.66 us (8%)
    pallas_call x1, Pallas kernels, tail_part(): pl.pallas_call(functools.partial(tail_kernel, heads, prompts, devices, gr...  69 us
    pallas_call x1, Pallas kernels, local_part(): pl.pallas_call(functools.partial(local_kernel, repeat, prompts), grid=(gr...  23.3 us
    unnamed x18, local copies, waits for them, and re-layouts  8.58 us

profile of v2, /device:TPU:24, one launch (start us, length us, event | category | flops | bytes accessed | tf_op | source)
XLA Modules:
  0.0 102.3 jit_solution(8322385020284141542)
XLA Ops:
  0.6 0.0 copy-start.7
  0.7 0.7 broadcast_compare_fusion.1
  1.3 0.1 add_convert_fusion
  1.4 0.1 broadcast_in_dim.2.mask_ref
  1.5 0.0 copy-start.1
  1.5 1.2 %copy-done.1 = bf16[512,1024]{1,0:T(8,128)(2,1)S(1)} copy-done((bf16[512,1024]{1,0:T(8,128)(2,1)S(1)}, bf16[512,1024]{1,0:T(8,128)(2,1)}, u32[]{:S(2)}) %copy-start.1) | copy-done | bytes 1048600
  2.7 0.0 copy-start.2
  2.7 1.0 %copy-done.2 = bf16[512,512]{1,0:T(8,128)(2,1)S(1)} copy-done((bf16[512,512]{1,0:T(8,128)(2,1)S(1)}, bf16[512,512]{1,0:T(8,128)(2,1)}, u32[]{:S(2)}) %copy-start.2) | copy-done | bytes 524312
  3.7 0.0 copy-start.3
  3.7 1.0 %copy-done.3 = bf16[512,512]{1,0:T(8,128)(2,1)S(1)} copy-done((bf16[512,512]{1,0:T(8,128)(2,1)S(1)}, bf16[512,512]{1,0:T(8,128)(2,1)}, u32[]{:S(2)}) %copy-start.3) | copy-done | bytes 524312
  4.8 0.0 copy-start.4
  4.8 0.7 copy-done.4
  5.5 0.0 copy-start.5
  5.5 0.7 copy-done.5
  6.2 0.0 copy-start.6
  6.2 0.7 copy-done.6
  6.9 23.3 %shard_map.104 = (f32[512,1024]{1,0:T(8,128)}, bf16[512,1024]{1,0:T(8,128)(2,1)S(1)}, f32[8,128,128]{2,1,0:T(8,128)S(1)}, bf16[8,128,128]{2,1,0:T(8,128)(2,1)S(1...) custom-call(s32[4]{0:T(128)S(1)} %copy-done.6, bf16[512,512]{1,0:T(8,128)(2,1)S(1)} %copy-done.2, ...), custom_call_target="tpu_custom_call" | custom-call | tf_op jit(solution)/shard_map/pallas_call | solution.py:196
  30.2 0.0 copy-done.7
  30.2 0.0 copy-start
  30.2 1.6 %copy-done = f32[512,1024]{1,0:T(8,128)S(1)} copy-done((f32[512,1024]{1,0:T(8,128)S(1)}, f32[512,1024]{1,0:T(8,128)}, u32[]{:S(2)}) %copy-start) | copy-done | bytes 2097176
  31.7 69.0 %shard_map.105 = (bf16[512,512]{1,0:T(8,128)(2,1)S(1)}, f32[1,8,128,128]{3,2,1,0:T(8,128)S(1)}) custom-call(f32[8,128,128]{2,1,0:T(8,128)S(1)} %get-tuple-element.8.l_ref, bf16[8,128,128]{2,1,0:T(8,128)(2,1)S(1)} %get-tuple-element.9.m_ref, f32[8,1,128]{2,1,0:T(1,128)S(1)} %broadcast_in_dim.2.mask_ref, f32[1,128]{1,0:T(1,128)S(1)} %bitcast.1, ...), custom_call_target="tpu_custom_call" | custom-call | tf_op jit(solution)/shard_map/pallas_call | solution.py:483
  100.7 0.8 copy.13
  101.5 0.8 copy.14
Async XLA Ops:
  0.6 29.5 %copy-start.7 = (f32[128]{0:T(128)S(1)}, f32[128]{0:T(128)}, u32[]{:S(2)}) copy-start(f32[128]{0:T(128)} %param.16) | copy-start | bytes 1540
  1.5 1.2 %copy-start.1 = (bf16[512,1024]{1,0:T(8,128)(2,1)S(1)}, bf16[512,1024]{1,0:T(8,128)(2,1)}, u32[]{:S(2)}) copy-start(bf16[512,1024]{1,0:T(8,128)(2,1)} %v_ref.1) | copy-start | bytes 3145732
  2.7 1.0 %copy-start.2 = (bf16[512,512]{1,0:T(8,128)(2,1)S(1)}, bf16[512,512]{1,0:T(8,128)(2,1)}, u32[]{:S(2)}) copy-start(bf16[512,512]{1,0:T(8,128)(2,1)} %q_ref.1) | copy-start | bytes 1572868
  3.7 1.0 %copy-start.3 = (bf16[512,512]{1,0:T(8,128)(2,1)S(1)}, bf16[512,512]{1,0:T(8,128)(2,1)}, u32[]{:S(2)}) copy-start(bf16[512,512]{1,0:T(8,128)(2,1)} %k_ref.1) | copy-start | bytes 1572868
  4.8 0.7 copy-start.4
  5.5 0.7 copy-start.5
  6.2 0.7 copy-start.6
  30.2 1.6 %copy-start = (f32[512,1024]{1,0:T(8,128)S(1)}, f32[512,1024]{1,0:T(8,128)}, u32[]{:S(2)}) copy-start(f32[512,1024]{1,0:T(8,128)} %get-tuple-element.10.o_hbm) | copy-start | bytes 6291460

commit v3 on v2

--- a/solution.py
+++ b/solution.py
@@ -30,14 +30,20 @@
 
 
 def local_kernel(
-    repeat, prompts, ps_ref, q_ref, k_ref, v_ref, gate_ref, rate_ref,
-    o_ref, y_ref, l_ref, m_ref, cl_ref, cm_ref,
+    repeat, prompts, ps_ref, owner_ref, q_ref, k_ref, v_ref, gate_ref, rate_ref,
+    o_ref, y_ref, l_ref, m_ref, cl_ref, cm_ref, mask_ref,
 ):
     h = pl.program_id(0)
     rows = q_ref.shape[0]
     number = rows // STRETCH
     blocks = rows // PAIR
-    base = lax.axis_index("seq") * number
+    position = lax.axis_index("seq")
+    base = position * number
+    mate = position + 1 - 2 * lax.rem(position, 2)
+    for p in range(prompts):
+        for i, place in enumerate((position, mate)):
+            owned = jnp.where(owner_ref[p] == place, 1.0, 0.0).astype(F32)
+            mask_ref[i * prompts + p] = jnp.full((1, DV), owned, F32)
     ri = lax.broadcasted_iota(jnp.int32, (PAIR, PAIR), 0)
     ci = lax.broadcasted_iota(jnp.int32, (PAIR, PAIR), 1)
     same = (ri // STRETCH) == (ci // STRETCH)
@@ -185,7 +191,7 @@
         m_ref[r] = states[r][:, DV:].astype(BF)
 
 
-def local_part(queries, key_vectors, values, gate_log, write_rate, prompt_stretches):
+def local_part(queries, key_vectors, values, gate_log, write_rate, prompt_stretches, decode_owner):
     rows = queries.shape[0]
     heads = gate_log.shape[0]
     groups = queries.shape[1] // DK
@@ -197,6 +203,7 @@
         functools.partial(local_kernel, repeat, prompts),
         grid=(groups,),
         in_specs=[
+            pl.BlockSpec(memory_space=pltpu.SMEM),
             pl.BlockSpec(memory_space=pltpu.SMEM),
             pl.BlockSpec((rows, DK), lambda h: (0, h)),
             pl.BlockSpec((rows, DK), lambda h: (0, h)),
@@ -211,6 +218,7 @@
             pl.BlockSpec((repeat, DK, DK), lambda h: (h, 0, 0)),
             pl.BlockSpec((prompts, repeat, DK, DV), lambda h: (0, h, 0, 0)),
             pl.BlockSpec((prompts, repeat, DK, DK), lambda h: (0, h, 0, 0)),
+            pl.BlockSpec((2 * prompts, 1, DV), lambda h: (0, 0, 0)),
         ],
         out_shape=[
             jax.ShapeDtypeStruct((rows, heads * DV), F32),
@@ -219,9 +227,10 @@
             jax.ShapeDtypeStruct((heads, DK, DK), BF),
             jax.ShapeDtypeStruct((prompts, heads, DK, DV), F32),
             jax.ShapeDtypeStruct((prompts, heads, DK, DK), BF),
+            jax.ShapeDtypeStruct((2 * prompts, 1, DV), F32),
         ],
-        compiler_params=pltpu.CompilerParams(vmem_limit_bytes=48 * 1024 * 1024),
-    )(prompt_stretches, queries, key_vectors, values, gate_log, write_rate)
+        compiler_params=pltpu.CompilerParams(vmem_limit_bytes=60 * 1024 * 1024),
+    )(prompt_stretches, decode_owner, queries, key_vectors, values, gate_log, write_rate)
 
 
 def tail_kernel(
@@ -235,7 +244,6 @@
 ):
     pos = lax.axis_index("seq")
     head = lax.axis_index("head")
-    half = prompts // 2
     xs = groups // 2
     here, core = head // 2, lax.rem(head, 2)
     side = lax.rem(pos, 2)
@@ -283,14 +291,18 @@
     def chain(h):
         return remote(nxt.at[h], inc.at[h], chain_s.at[h], chain_r.at[h], seq=right)
 
-    def pair(h):
-        return remote(pair_out.at[h], pair_in.at[h], pair_s.at[h], pair_r.at[h], seq=mate)
-
-    def upward(h):
-        return remote(up_out.at[h], up_in.at[h], up_s.at[h], up_r.at[h], seq=above)
-
-    def downward(h):
-        return remote(down_out.at[h], down_in.at[h], down_s.at[h], down_r.at[h], seq=below)
+    def pair(i, h):
+        return remote(
+            pair_out.at[i, h], pair_in.at[i, h], pair_s.at[i, h], pair_r.at[i, h], seq=mate
+        )
+
+    def upward(i, h):
+        return remote(up_out.at[i, h], up_in.at[i, h], up_s.at[i, h], up_r.at[i, h], seq=above)
+
+    def downward(i, h):
+        return remote(
+            down_out.at[i, h], down_in.at[i, h], down_s.at[i, h], down_r.at[i, h], seq=below
+        )
 
     def deliver(h):
         return remote(sel_out.at[h], sel_in.at[h], sel_s.at[h], sel_r.at[h], seq=mate)
@@ -305,40 +317,70 @@
             x_out.at[k - 1], x_in.at[k - 1], x_s.at[k - 1], x_r.at[k - 1], head=x_heads[k - 1]
         )
 
+    middle = devices // 2
+    odd, even = side == 1, side == 0
+    last = pos == devices - 1
+    low = pos < middle
+    pair_sends = [odd | (pos >= middle - 1), odd & low]
+    pair_takes = [even | (mate >= middle - 1), even & (mate < middle)]
+    up_sends = [has_above, has_above & even]
+    up_takes = [has_below, has_below & even]
+    down_sends = [has_below, has_below & (odd | low)]
+    down_takes = [has_above, has_above & (odd | (pos + 2 < middle))]
+    kept_prompt = [1 + side, 3 * side]
+    mate_prompt = [2 - side, 3 - 3 * side]
+
     @pl.when(pos == 0)
     def _():
         inc[...] = jnp.zeros_like(inc)
+
+    for i in range(2):
+        @pl.when(jnp.logical_not(up_takes[i]))
+        def _(i=i):
+            up_in[i] = jnp.zeros(up_in.shape[1:], BF)
+
+        @pl.when(jnp.logical_not(down_takes[i]))
+        def _(i=i):
+            down_in[i] = jnp.zeros(down_in.shape[1:], BF)
+
+    loads[0].wait()
+    loads[1].wait()
+
+    def table(p, h):
+        return (cl_ref[p, h] + mm(cm_ref[p, h], inc[h])).astype(BF)
+
+    def table_step(h, _):
+        for i in range(2):
+            @pl.when(pair_sends[i])
+            def _(i=i):
+                pair_out[i, h] = table(mate_prompt[i], h)
+                pair(i, h).start()
+
+        for i in range(2):
+            own[i, h] = table(kept_prompt[i], h)
+        return 0
 
     def chain_step(h, _):
         @pl.when(has_left)
         def _():
             chain(h).wait_recv()
 
-        nxt[h] = (mm(m_ref[h], inc[h]) + l_ref[h]).astype(BF)
-
         @pl.when(has_right)
         def _():
+            nxt[h] = (mm(m_ref[h], inc[h]) + l_ref[h]).astype(BF)
             chain(h).start()
 
+        @pl.when(last)
+        def _():
+            table_step(h, 0)
+
         return 0
 
     lax.fori_loop(0, heads, chain_step, 0)
 
-    loads[0].wait()
-    loads[1].wait()
-
-    def table(p, h):
-        return (cl_ref[p, h] + mm(cm_ref[p, h], inc[h])).astype(BF)
-
-    def pair_step(h, _):
-        for i in range(half):
-            pair_out[h, i] = table((1 - side) * half + i, h)
-        pair(h).start()
-        for i in range(half):
-            own[h, i] = table(side * half + i, h)
-        return 0
-
-    lax.fori_loop(0, heads, pair_step, 0)
+    @pl.when(has_right)
+    def _():
+        lax.fori_loop(0, heads, table_step, 0)
 
     loads[2].wait()
     loads[3].wait()
@@ -355,8 +397,7 @@
         w = w_ref[:, pl.ds(pl.multiple_of(slot * cols, 128), cols)]
         return mm(hid[...], w)
 
-    order = list(range(1, xs)) + [0]
-    for k in order:
+    for k in range(1, xs):
         core_out[k] = project(k, 1 - core).astype(BF)
         to_core(k).start()
     for k in range(1, xs):
@@ -366,70 +407,78 @@
         to_x(k).start()
 
     def gather_step(h, _):
-        pair(h).wait_recv()
-        own[h] = own[h] + pair_in[h]
-        return 0
-
-    lax.fori_loop(0, heads, gather_step, 0)
-
-    @pl.when(pos < 2)
-    def _():
-        up_in[...] = jnp.zeros_like(up_in)
-
-    @pl.when(pos >= devices - 2)
-    def _():
-        down_in[...] = jnp.zeros_like(down_in)
+        for i in range(2):
+            @pl.when(pair_takes[i])
+            def _(i=i):
+                pair(i, h).wait_recv()
+                own[i, h] = own[i, h] + pair_in[i, h]
+
+        return 0
 
     def up_step(h, _):
-        @pl.when(has_below)
-        def _():
-            upward(h).wait_recv()
-
-        @pl.when(has_above)
-        def _():
-            up_out[h] = up_in[h] + own[h]
-            upward(h).start()
+        for i in range(2):
+            @pl.when(up_takes[i])
+            def _(i=i):
+                upward(i, h).wait_recv()
+
+            @pl.when(up_sends[i])
+            def _(i=i):
+                up_out[i, h] = up_in[i, h] + own[i, h]
+                upward(i, h).start()
 
         return 0
 
     def down_step(h, _):
-        @pl.when(has_above)
-        def _():
-            downward(h).wait_recv()
-
-        @pl.when(has_below)
-        def _():
-            down_out[h] = down_in[h] + own[h]
-            downward(h).start()
-
-        return 0
-
-    low = pos < devices // 2
-
-    @pl.when(low)
-    def _():
-        lax.fori_loop(0, heads, up_step, 0)
-        lax.fori_loop(0, heads, down_step, 0)
-
-    @pl.when(jnp.logical_not(low))
-    def _():
-        lax.fori_loop(0, heads, down_step, 0)
-        lax.fori_loop(0, heads, up_step, 0)
+        for i in range(2):
+            @pl.when(down_takes[i])
+            def _(i=i):
+                downward(i, h).wait_recv()
+
+            @pl.when(down_sends[i])
+            def _(i=i):
+                down_out[i, h] = down_in[i, h] + own[i, h]
+                downward(i, h).start()
+
+        return 0
 
     def select_step(h, _):
         kept = jnp.zeros((DK, DV), F32)
         sent = jnp.zeros((DK, DV), F32)
-        for i in range(half):
-            full = (up_in[h, i] + own[h, i] + down_in[h, i]).astype(F32)
-            p = side * half + i
-            kept = kept + full * mask_ref[p]
-            sent = sent + full * mask_ref[prompts + p]
+        for i in range(2):
+            full = (up_in[i, h] + own[i, h] + down_in[i, h]).astype(F32)
+            kept = kept + full * mask_ref[kept_prompt[i]]
+            sent = sent + full * mask_ref[prompts + kept_prompt[i]]
         sel_out[h] = sent.astype(BF)
         deliver(h).start()
         owned_ref[0, h] = kept
         return 0
 
-    lax.fori_loop(0, heads, select_step, 0)
+    def both(*steps):
+        def run(h, _):
+            for step in steps:
+                step(h, 0)
+            return 0
+
+        lax.fori_loop(0, heads, run, 0)
+
+    @pl.when(low)
+    def _():
+        both(gather_step, up_step)
+
+    @pl.when(jnp.logical_not(low))
+    def _():
+        both(gather_step, down_step)
+
+    core_out[0] = project(0, 1 - core).astype(BF)
+    to_core(0).start()
+
+    @pl.when(low)
+    def _():
+        both(down_step, select_step)
+
+    @pl.when(jnp.logical_not(low))
+    def _():
+        both(up_step, select_step)
 
     mine = project(0, core)
     to_core(0).wait_recv()
@@ -442,20 +491,17 @@
     def last_step(h, _):
         deliver(h).wait_recv()
         owned_ref[0, h] = owned_ref[0, h] + sel_in[h].astype(F32)
-        pair(h).wait_send()
         deliver(h).wait_send()
 
         @pl.when(has_right)
         def _():
             chain(h).wait_send()
 
-        @pl.when(has_above)
-        def _():
-            upward(h).wait_send()
-
-        @pl.when(has_below)
-        def _():
-            downward(h).wait_send()
+        for i in range(2):
+            for sends, copy in ((pair_sends, pair), (up_sends, upward), (down_sends, downward)):
+                @pl.when(sends[i])
+                def _(i=i, copy=copy):
+                    copy(i, h).wait_send()
 
         return 0
 
@@ -470,7 +516,7 @@
     rows, width = o_loc.shape
     heads = width // DV
     prompts = close_l.shape[0]
-    half = prompts // 2
+    assert prompts == 4
     devices = lax.axis_size("seq")
     groups = lax.axis_size("head")
     xs = groups // 2
@@ -478,7 +524,7 @@
     vmem = pl.BlockSpec(memory_space=pltpu.VMEM)
     anywhere = pl.BlockSpec(memory_space=pl.ANY)
     dma = pltpu.SemaphoreType.DMA
-    line = pltpu.VMEM((heads, half, DK, DV), BF)
+    line = pltpu.VMEM((2, heads, DK, DV), BF)
     state = pltpu.VMEM((heads, DK, DV), BF)
     return pl.pallas_call(
         functools.partial(tail_kernel, heads, prompts, devices, groups),
@@ -501,7 +547,7 @@
             pltpu.VMEM((xs - 1, rows, cols), BF),
             pltpu.VMEM((xs - 1, rows, cols), BF),
             dma((5,)),
-        ] + [dma((heads,))] * 10 + [dma((xs,))] * 2 + [dma((xs - 1,))] * 2,
+        ] + [dma((heads,))] * 2 + [dma((2, heads))] * 6 + [dma((heads,))] * 2 + [dma((xs,))] * 2 + [dma((xs - 1,))] * 2,
         compiler_params=pltpu.CompilerParams(
             collective_id=0, has_side_effects=True, vmem_limit_bytes=48 * 1024 * 1024
         ),
@@ -515,13 +561,9 @@
     queries, key_vectors, values, gate_log, write_rate,
     prompt_stretches, decode_owner, norm_gain, out_weight,
 ):
-    position = lax.axis_index("seq")
-    o_loc, y_map, local_state, local_map, close_l, close_m = local_part(
-        queries, key_vectors, values, gate_log, write_rate, prompt_stretches
+    o_loc, y_map, local_state, local_map, close_l, close_m, masks = local_part(
+        queries, key_vectors, values, gate_log, write_rate, prompt_stretches, decode_owner
     )
-    mate = position + 1 - 2 * (position % 2)
-    masks = jnp.concatenate([decode_owner == position, decode_owner == mate]).astype(F32)
-    masks = jnp.broadcast_to(masks[:, None, None], (masks.shape[0], 1, DV))
     return tail_part(
         local_state, local_map, masks, norm_gain, o_loc, y_map, close_l, close_m, out_weight
     )

time: 103 us -> 91.9 us (0.89)
  the two profiles are of different devices: /device:TPU:24 before, /device:TPU:0 now
where the time goes in v3:
time: 91.9 us; the launch traced here: 91.5 us
  Pallas kernels  82.6 us (90%)
  local copies, waits for them, and re-layouts  8.29 us (9%)
    pallas_call x1, Pallas kernels, tail_part(): pl.pallas_call(functools.partial(tail_kernel, heads, prompts, devices, gr...  58.7 us
    pallas_call x1, Pallas kernels, local_part(): pl.pallas_call(functools.partial(local_kernel, repeat, prompts), grid=(gr...  23.9 us
    unnamed x16, local copies, waits for them, and re-layouts  8.29 us

profile of v3, /device:TPU:0, one launch (start us, length us, event | category | flops | bytes accessed | tf_op | source)
XLA Modules:
  0.0 91.5 jit_solution(4258060679233348822)
XLA Ops:
  0.6 0.0 copy-start.6
  0.6 23.9 %shard_map.104 = (f32[512,1024]{1,0:T(8,128)}, bf16[512,1024]{1,0:T(8,128)(2,1)}, f32[8,128,128]{2,1,0:T(8,128)}, bf16[8,128,128]{2,1,0:T(8,128)(2,1)}, f32[4,8,...) custom-call(s32[4]{0:T(128)} %ps_ref.1, s32[4]{0:T(128)} %owner_ref.1, ...), custom_call_target="tpu_custom_call" | custom-call | tf_op jit(solution)/shard_map/pallas_call | solution.py:202
  24.5 0.0 copy-done.6
  24.5 0.0 copy-start
  24.5 1.6 %copy-done = f32[512,1024]{1,0:T(8,128)S(1)} copy-done((f32[512,1024]{1,0:T(8,128)S(1)}, f32[512,1024]{1,0:T(8,128)}, u32[]{:S(2)}) %copy-start) | copy-done | bytes 2097176
  26.1 0.0 copy-start.1
  26.1 1.2 %copy-done.1 = bf16[512,1024]{1,0:T(8,128)(2,1)S(1)} copy-done((bf16[512,1024]{1,0:T(8,128)(2,1)S(1)}, bf16[512,1024]{1,0:T(8,128)(2,1)}, u32[]{:S(2)}) %copy-start.1) | copy-done | bytes 1048600
  27.4 0.0 copy-start.2
  27.4 1.2 %copy-done.2 = bf16[4,8,128,128]{3,2,1,0:T(8,128)(2,1)S(1)} copy-done((bf16[4,8,128,128]{3,2,1,0:T(8,128)(2,1)S(1)}, bf16[4,8,128,128]{3,2,1,0:T(8,128)(2,1)}, u32[]{:S(2)}) %copy-start.2) | copy-done | bytes 1048600
  28.6 0.0 copy-start.3
  28.6 1.0 %copy-done.3 = f32[8,128,128]{2,1,0:T(8,128)S(1)} copy-done((f32[8,128,128]{2,1,0:T(8,128)S(1)}, f32[8,128,128]{2,1,0:T(8,128)}, u32[]{:S(2)}) %copy-start.3) | copy-done | bytes 524312
  29.6 0.0 copy-start.4
  29.6 0.9 %copy-done.4 = bf16[8,128,128]{2,1,0:T(8,128)(2,1)S(1)} copy-done((bf16[8,128,128]{2,1,0:T(8,128)(2,1)S(1)}, bf16[8,128,128]{2,1,0:T(8,128)(2,1)}, u32[]{:S(2)}) %copy-start.4) | copy-done | bytes 262168
  30.6 0.0 copy-start.5
  30.6 0.7 copy-done.5
  31.3 58.7 %shard_map.105 = (bf16[512,512]{1,0:T(8,128)(2,1)S(1)}, f32[1,8,128,128]{3,2,1,0:T(8,128)S(1)}) custom-call(f32[8,128,128]{2,1,0:T(8,128)S(1)} %copy-done.3, bf16[8,128,128]{2,1,0:T(8,128)(2,1)S(1)} %copy-done.4, f32[8,1,128]{2,1,0:T(1,128)S(1)} %copy-done.5, f32[1,128]{1,0:T(1,128)S(1)} %bitcast.1, f32[512,1024]{1,0:T(8,128)S(1)} %copy-done, ...), custom_call_target="tpu_custom_call" | custom-call | tf_op jit(solution)/shard_map/pallas_call | solution.py:529
  89.9 0.8 copy.13
  90.7 0.8 copy.14
Async XLA Ops:
  0.6 23.9 %copy-start.6 = (f32[128]{0:T(128)S(1)}, f32[128]{0:T(128)}, u32[]{:S(2)}) copy-start(f32[128]{0:T(128)} %param.16) | copy-start | bytes 1540
  24.5 1.6 %copy-start = (f32[512,1024]{1,0:T(8,128)S(1)}, f32[512,1024]{1,0:T(8,128)}, u32[]{:S(2)}) copy-start(f32[512,1024]{1,0:T(8,128)} %get-tuple-element.12.o_hbm) | copy-start | bytes 6291460
  26.1 1.2 %copy-start.1 = (bf16[512,1024]{1,0:T(8,128)(2,1)S(1)}, bf16[512,1024]{1,0:T(8,128)(2,1)}, u32[]{:S(2)}) copy-start(bf16[512,1024]{1,0:T(8,128)(2,1)} %get-tuple-element.13.y_hbm) | copy-start | bytes 3145732
  27.4 1.2 %copy-start.2 = (bf16[4,8,128,128]{3,2,1,0:T(8,128)(2,1)S(1)}, bf16[4,8,128,128]{3,2,1,0:T(8,128)(2,1)}, u32[]{:S(2)}) copy-start(bf16[4,8,128,128]{3,2,1,0:T(8,128)(2,1)} %get-tuple-element.15.cm_hbm) | copy-start | bytes 3145732
  28.6 1.0 %copy-start.3 = (f32[8,128,128]{2,1,0:T(8,128)S(1)}, f32[8,128,128]{2,1,0:T(8,128)}, u32[]{:S(2)}) copy-start(f32[8,128,128]{2,1,0:T(8,128)} %get-tuple-element.9.l_ref) | copy-start | bytes 1572868
  29.6 0.9 %copy-start.4 = (bf16[8,128,128]{2,1,0:T(8,128)(2,1)S(1)}, bf16[8,128,128]{2,1,0:T(8,128)(2,1)}, u32[]{:S(2)}) copy-start(bf16[8,128,128]{2,1,0:T(8,128)(2,1)} %get-tuple-element.10.m_ref) | copy-start | bytes 786436
  30.6 0.7 copy-start.5

commit v4 on v3

--- a/solution.py
+++ b/solution.py
@@ -51,9 +51,8 @@
     strict_mask = same & (ri > ci)
     causal_mask = same & (ri >= ci)
     eye_f = eye.astype(F32)
-    eye_b = eye_f.astype(BF)
-    upto = (same & (ri <= ci)).astype(F32)
-    after = (same & (ri > ci)).astype(F32)
+    upto = (same & (ri <= ci)).astype(F32).astype(BF)
+    after = (same & (ri > ci)).astype(F32).astype(BF)
     first_half = lax.broadcasted_iota(jnp.int32, (PAIR, 1), 0) < STRETCH
 
     gram, scores0, keys, keys_t, qs, qscale = [], [], [], [], [], []
@@ -76,10 +75,20 @@
         qscale.append(lax.rsqrt(jnp.sum(qf * qf, axis=1, keepdims=True) + 1e-06) * DK ** (-0.5))
 
     grow_all, suf_all = [], []
+    sums = jnp.concatenate([upto, after], axis=1)
     for c in range(blocks):
         gate = gate_ref[:, c * PAIR:(c + 1) * PAIR]
-        grow_all.append(jnp.dot(gate, upto, preferred_element_type=F32, precision=HIGH))
-        suf_all.append(jnp.dot(gate, after, preferred_element_type=F32, precision=HIGH))
+        g_hi = gate.astype(BF)
+        rest = gate - g_hi.astype(F32)
+        g_mid, g_lo = split(rest)
+        three = jnp.concatenate([g.astype(F32) for g in (g_hi, g_mid, g_lo)], axis=0)
+        summed = mm(three.astype(BF), sums)
+        n_heads = gate.shape[0]
+        summed = (
+            summed[:n_heads] + summed[n_heads:2 * n_heads] + summed[2 * n_heads:3 * n_heads]
+        )
+        grow_all.append(summed[:, :PAIR])
+        suf_all.append(summed[:, PAIR:])
     head_row = lax.broadcasted_iota(jnp.int32, (gate_ref.shape[0], PAIR), 0)
     items = [(c, r) for r in range(repeat) for c in range(blocks)]
     lower, inv, info = [], [], []
@@ -100,31 +109,33 @@
         inv.append(jnp.where(eye, 1.0, jnp.where((ri // 2) == (ci // 2), -a, 0.0)))
         info.append((grow, rate, gcol, sufcol, sc))
 
+    lower_b = [a.astype(BF) for a in lower]
     size = 2
     while size < STRETCH:
         off = ((ri // (2 * size)) == (ci // (2 * size))) & ((ri // size) != (ci // size))
+        off_b = off.astype(F32).astype(BF)
         invb = [t.astype(BF) for t in inv]
-        part = [
-            mm(jnp.where(off, a, 0.0).astype(BF), tb).astype(BF) for a, tb in zip(lower, invb)
-        ]
+        part = [mm(ab * off_b, tb).astype(BF) for ab, tb in zip(lower_b, invb)]
         inv = [t - mm(tb, p) for t, tb, p in zip(inv, invb, part)]
         size *= 2
 
-    solved = []
+    def twice(x, y, x_high=None):
+        high = x.astype(BF) if x_high is None else x_high
+        low = (x - high.astype(F32)).astype(BF)
+        product = mm(jnp.concatenate([high, low], axis=0), y)
+        return product[:PAIR] + product[PAIR:]
+
     invb = [t.astype(BF) for t in inv]
-    resid = []
-    for a, tb in zip(lower, invb):
-        hi, lo = split(a)
-        resid.append((eye_f - tb.astype(F32)) - (mm(hi, tb) + mm(lo, tb)))
+    resid = [
+        (eye_f - tb.astype(F32)) - twice(a, tb, ab) for a, ab, tb in zip(lower, lower_b, invb)
+    ]
     inv = [tb.astype(F32) + mm(tb, e.astype(BF)) for tb, e in zip(invb, resid)]
     wu = []
     for (c, r), t, (grow, rate, gcol, sufcol, sc) in zip(items, inv, info):
         sl = slice(c * PAIR, (c + 1) * PAIR)
         v = v_ref[sl, r * DV:(r + 1) * DV]
-        wh, wl = split(t * (rate * jnp.exp(grow) * rk_row[c]))
-        uh, ul = split(t * rate)
-        w = mm(wh, keys[c]) + mm(wl, keys[c])
-        u = mm(uh, v) + mm(ul, v)
+        w = twice(t * (rate * jnp.exp(grow) * rk_row[c]), keys[c])
+        u = twice(t * rate, v)
         wu.append((w, u))
     trans, qside = [], []
     for (c, r), (w, u), (grow, rate, gcol, sufcol, sc) in zip(items, wu, info):
@@ -235,9 +246,9 @@
 
 def tail_kernel(
     heads, prompts, devices, groups,
-    l_ref, m_ref, mask_ref, gain_ref, o_hbm, y_hbm, cl_hbm, cm_hbm, w_hbm,
+    l_hbm, m_hbm, mask_hbm, gain_hbm, o_hbm, y_hbm, cl_hbm, cm_hbm, w_hbm,
     mixed_ref, owned_ref,
-    o_ref, y_ref, cl_ref, cm_ref, w_ref, inc, nxt, pair_out, pair_in, own,
+    l_ref, m_ref, mask_ref, gain_ref, o_ref, y_ref, cl_ref, cm_ref, w_ref, inc, nxt, pair_out, pair_in, own,
     up_in, up_out, down_in, down_out, sel_out, sel_in, hid, core_out, core_in, x_out, x_in,
     load_sem, chain_s, chain_r, pair_s, pair_r, up_s, up_r, down_s, down_r,
     sel_s, sel_r, core_s, core_r, x_s, x_r,
@@ -255,7 +266,11 @@
     loads = [
         pltpu.make_async_copy(src, dst, load_sem.at[i])
         for i, (src, dst) in enumerate(
-            [(cl_hbm, cl_ref), (cm_hbm, cm_ref), (o_hbm, o_ref), (y_hbm, y_ref), (w_hbm, w_ref)]
+            [
+                (l_hbm, l_ref), (m_hbm, m_ref), (cl_hbm, cl_ref), (cm_hbm, cm_ref),
+                (o_hbm, o_ref), (y_hbm, y_ref), (w_hbm, w_ref), (mask_hbm, mask_ref),
+                (gain_hbm, gain_ref),
+            ]
         )
     ]
     for load in loads:
@@ -346,6 +361,11 @@
     loads[0].wait()
     loads[1].wait()
 
+    @pl.when(last)
+    def _():
+        loads[2].wait()
+        loads[3].wait()
+
     def table(p, h):
         return (cl_ref[p, h] + mm(cm_ref[p, h], inc[h])).astype(BF)
 
@@ -373,6 +393,8 @@
         @pl.when(last)
         def _():
             table_step(h, 0)
+            down_out[1, h] = own[1, h]
+            downward(1, h).start()
 
         return 0
 
@@ -380,31 +402,22 @@
 
     @pl.when(has_right)
     def _():
+        loads[2].wait()
+        loads[3].wait()
         lax.fori_loop(0, heads, table_step, 0)
 
-    loads[2].wait()
-    loads[3].wait()
+    for load in loads[4:6] + loads[7:]:
+        load.wait()
     gain = gain_ref[...]
     for j in range(heads):
         cs = slice(j * DV, (j + 1) * DV)
         out = o_ref[:, cs] + mm(y_ref[:, cs], inc[j])
         mean = jnp.mean(out * out, axis=1, keepdims=True)
         hid[:, cs] = (out * lax.rsqrt(mean + 1e-06) * gain).astype(BF)
-    loads[4].wait()
-
     def project(k, which):
         slot = lax.rem(here + k, xs) * 2 + which
         w = w_ref[:, pl.ds(pl.multiple_of(slot * cols, 128), cols)]
         return mm(hid[...], w)
-
-    for k in range(1, xs):
-        core_out[k] = project(k, 1 - core).astype(BF)
-        to_core(k).start()
-    for k in range(1, xs):
-        mine = project(k, core)
-        to_core(k).wait_recv()
-        x_out[k - 1] = (mine + core_in[k].astype(F32)).astype(BF)
-        to_x(k).start()
 
     def gather_step(h, _):
         for i in range(2):
@@ -434,7 +447,7 @@
             def _(i=i):
                 downward(i, h).wait_recv()
 
-            @pl.when(down_sends[i])
+            @pl.when(down_sends[i] & (has_right if i == 1 else has_below))
             def _(i=i):
                 down_out[i, h] = down_in[i, h] + own[i, h]
                 downward(i, h).start()
@@ -468,6 +481,16 @@
     @pl.when(jnp.logical_not(low))
     def _():
         both(gather_step, down_step)
+
+    loads[6].wait()
+    for k in range(1, xs):
+        core_out[k] = project(k, 1 - core).astype(BF)
+        to_core(k).start()
+    for k in range(1, xs):
+        mine = project(k, core)
+        to_core(k).wait_recv()
+        x_out[k - 1] = (mine + core_in[k].astype(F32)).astype(BF)
+        to_x(k).start()
 
     core_out[0] = project(0, 1 - core).astype(BF)
     to_core(0).start()
@@ -528,13 +551,17 @@
     state = pltpu.VMEM((heads, DK, DV), BF)
     return pl.pallas_call(
         functools.partial(tail_kernel, heads, prompts, devices, groups),
-        in_specs=[vmem] * 4 + [anywhere] * 5,
+        in_specs=[anywhere] * 9,
         out_specs=[vmem, vmem],
         out_shape=[
             jax.ShapeDtypeStruct((rows, cols), BF),
             jax.ShapeDtypeStruct((1, heads, DK, DV), F32),
         ],
         scratch_shapes=[
+            pltpu.VMEM(local_state.shape, F32),
+            pltpu.VMEM(local_map.shape, BF),
+            pltpu.VMEM(masks.shape, F32),
+            pltpu.VMEM((1, DV), F32),
             pltpu.VMEM(o_loc.shape, F32),
             pltpu.VMEM(y_map.shape, BF),
             pltpu.VMEM(close_l.shape, F32),
@@ -546,10 +573,10 @@
             pltpu.VMEM((xs, rows, cols), BF),
             pltpu.VMEM((xs - 1, rows, cols), BF),
             pltpu.VMEM((xs - 1, rows, cols), BF),
-            dma((5,)),
+            dma((9,)),
         ] + [dma((heads,))] * 2 + [dma((2, heads))] * 6 + [dma((heads,))] * 2 + [dma((xs,))] * 2 + [dma((xs - 1,))] * 2,
         compiler_params=pltpu.CompilerParams(
-            collective_id=0, has_side_effects=True, vmem_limit_bytes=48 * 1024 * 1024
+            collective_id=0, has_side_effects=True, vmem_limit_bytes=60 * 1024 * 1024
         ),
     )(
         local_state, local_map, masks, norm_gain.reshape(1, -1),

time: 91.9 us -> 83.1 us (0.904)
  the two profiles are of different devices: /device:TPU:0 before, /device:TPU:29 now
where the time goes in v4:
time: 83.1 us; the launch traced here: 82.9 us
  Pallas kernels  78.5 us (94%)
  local copies, waits for them, and re-layouts  3.74 us (5%)
    pallas_call x1, Pallas kernels, tail_part(): pl.pallas_call(functools.partial(tail_kernel, heads, prompts, devices, gr...  55.1 us
    pallas_call x1, Pallas kernels, local_part(): pl.pallas_call(functools.partial(local_kernel, repeat, prompts), grid=(gr...  23.4 us
    unnamed x2, local copies, waits for them, and re-layouts  3.74 us

profile of v4, /device:TPU:29, one launch (start us, length us, event | category | flops | bytes accessed | tf_op | source)
XLA Modules:
  0.0 82.9 jit_solution(18358948868059276477)
XLA Ops:
  0.6 23.4 %shard_map.104 = (f32[512,1024]{1,0:T(8,128)}, bf16[512,1024]{1,0:T(8,128)(2,1)}, f32[8,128,128]{2,1,0:T(8,128)}, bf16[8,128,128]{2,1,0:T(8,128)(2,1)}, f32[4,8,...) custom-call(s32[4]{0:T(128)} %ps_ref.1, s32[4]{0:T(128)} %owner_ref.1, ...), custom_call_target="tpu_custom_call" | custom-call | tf_op jit(solution)/shard_map/pallas_call | solution.py:213
  24.0 55.1 %shard_map.105 = (bf16[512,512]{1,0:T(8,128)(2,1)}, f32[1,8,128,128]{3,2,1,0:T(8,128)}) custom-call(f32[8,128,128]{2,1,0:T(8,128)} %get-tuple-element.9.l_hbm, bf16[8,128,128]{2,1,0:T(8,128)(2,1)} %get-tuple-element.10.m_hbm, f32[8,1,128]{2,1,0:T(1,128)} %get-tuple-element.11.mask_hbm, f32[1,128]{1,0:T(1,128)} %bitcast.1, ...), custom_call_target="tpu_custom_call" | custom-call | tf_op jit(solution)/shard_map/pallas_call | solution.py:552
  79.2 1.9 %copy.13 = bf16[512,512]{1,0:T(8,128)(2,1)} copy(bf16[512,512]{1,0:T(8,128)(2,1)} %get-tuple-element.18) | data formatting | bytes 1048576
  81.0 1.9 %copy.14 = f32[1,8,128,128]{3,2,1,0:T(8,128)} copy(f32[1,8,128,128]{3,2,1,0:T(8,128)} %get-tuple-element.19) | data formatting | bytes 1048576

commit v5 on v4

--- a/solution.py
+++ b/solution.py
@@ -406,7 +406,7 @@
         loads[3].wait()
         lax.fori_loop(0, heads, table_step, 0)
 
-    for load in loads[4:6] + loads[7:]:
+    for load in loads[4:]:
         load.wait()
     gain = gain_ref[...]
     for j in range(heads):
@@ -474,32 +474,32 @@
 
         lax.fori_loop(0, heads, run, 0)
 
-    @pl.when(low)
-    def _():
-        both(gather_step, up_step)
-
-    @pl.when(jnp.logical_not(low))
-    def _():
-        both(gather_step, down_step)
-
-    loads[6].wait()
+    up_first = pos < devices - 2
     for k in range(1, xs):
         core_out[k] = project(k, 1 - core).astype(BF)
         to_core(k).start()
+
+    @pl.when(up_first)
+    def _():
+        both(gather_step, up_step)
+
+    @pl.when(jnp.logical_not(up_first))
+    def _():
+        both(gather_step, down_step)
+
     for k in range(1, xs):
         mine = project(k, core)
         to_core(k).wait_recv()
         x_out[k - 1] = (mine + core_in[k].astype(F32)).astype(BF)
         to_x(k).start()
-
     core_out[0] = project(0, 1 - core).astype(BF)
     to_core(0).start()
 
-    @pl.when(low)
+    @pl.when(up_first)
     def _():
         both(down_step, select_step)
 
-    @pl.when(jnp.logical_not(low))
+    @pl.when(jnp.logical_not(up_first))
     def _():
         both(up_step, select_step)
 
@@ -584,6 +584,29 @@
     )
 
 
+def copy_kernel(a_ref, b_ref, a_out, b_out, sems):
+    copies = [
+        pltpu.make_async_copy(a_ref, a_out, sems.at[0]),
+        pltpu.make_async_copy(b_ref, b_out, sems.at[1]),
+    ]
+    for copy in copies:
+        copy.start()
+    for copy in copies:
+        copy.wait()
+
+
+def copied(a, b):
+    anywhere = pl.BlockSpec(memory_space=pl.ANY)
+    return pl.pallas_call(
+        copy_kernel,
+        in_specs=[anywhere, anywhere],
+        out_specs=[anywhere, anywhere],
+        out_shape=[jax.ShapeDtypeStruct(a.shape, a.dtype), jax.ShapeDtypeStruct(b.shape, b.dtype)],
+        scratch_shapes=[pltpu.SemaphoreType.DMA((2,))],
+        compiler_params=pltpu.CompilerParams(vmem_limit_bytes=60 * 1024 * 1024),
+    )(a, b)
+
+
 def body(
     queries, key_vectors, values, gate_log, write_rate,
     prompt_stretches, decode_owner, norm_gain, out_weight,
@@ -591,9 +614,10 @@
     o_loc, y_map, local_state, local_map, close_l, close_m, masks = local_part(
         queries, key_vectors, values, gate_log, write_rate, prompt_stretches, decode_owner
     )
-    return tail_part(
+    mixed, owned = tail_part(
         local_state, local_map, masks, norm_gain, o_loc, y_map, close_l, close_m, out_weight
     )
+    return copied(mixed, owned)
 
 
 def solution(mesh):

time: 83.1 us -> 111 us (1.34)
  the two profiles are of different devices: /device:TPU:29 before, /device:TPU:0 now
where the time goes in v5:
time: 111 us
  Pallas kernels  110 us (99%)
    pallas_call x1, Pallas kernels, tail_part(): pl.pallas_call(functools.partial(tail_kernel, heads, prompts, devices, gr...  53.9 us
    pallas_call x1, Pallas kernels, copied(): pl.pallas_call(copy_kernel, in_specs=[anywhere, anywhere], out_specs=[any...  32.9 us
    pallas_call x1, Pallas kernels, local_part(): pl.pallas_call(functools.partial(local_kernel, repeat, prompts), grid=(gr...  23.4 us

profile of v5, /device:TPU:0, one launch (start us, length us, event | category | flops | bytes accessed | tf_op | source)
XLA Modules:
  0.0 110.8 jit_solution(17778093691661882922)
XLA Ops:
  0.6 23.4 %shard_map.104 = (f32[512,1024]{1,0:T(8,128)}, bf16[512,1024]{1,0:T(8,128)(2,1)}, f32[8,128,128]{2,1,0:T(8,128)}, bf16[8,128,128]{2,1,0:T(8,128)(2,1)}, f32[4,8,...) custom-call(s32[4]{0:T(128)} %ps_ref.1, s32[4]{0:T(128)} %owner_ref.1, ...), custom_call_target="tpu_custom_call" | custom-call | tf_op jit(solution)/shard_map/pallas_call | solution.py:213
  24.0 53.9 %shard_map.105 = (bf16[512,512]{1,0:T(8,128)(2,1)}, f32[1,8,128,128]{3,2,1,0:T(8,128)}) custom-call(f32[8,128,128]{2,1,0:T(8,128)} %get-tuple-element.11.l_hbm, bf16[8,128,128]{2,1,0:T(8,128)(2,1)} %get-tuple-element.12.m_hbm, f32[8,1,128]{2,1,0:T(1,128)} %get-tuple-element.13.mask_hbm, f32[1,128]{1,0:T(1,128)} %bitcast.1, ...), custom_call_target="tpu_custom_call" | custom-call | tf_op jit(solution)/shard_map/pallas_call | solution.py:552
  77.9 32.9 %shard_map.106 = (bf16[512,512]{1,0:T(8,128)(2,1)}, f32[1,8,128,128]{3,2,1,0:T(8,128)}) custom-call(bf16[512,512]{1,0:T(8,128)(2,1)} %get-tuple-element.18.a_ref, f32[1,8,128,128]{3,2,1,0:T(8,128)} %get-tuple-element.19.b_ref), custom_call_target="tpu_custom_call" | custom-call | tf_op jit(solution)/shard_map/pallas_call | solution.py:600

commit v6 on v5

--- a/solution.py
+++ b/solution.py
@@ -584,25 +584,22 @@
     )
 
 
-def copy_kernel(a_ref, b_ref, a_out, b_out, sems):
-    copies = [
-        pltpu.make_async_copy(a_ref, a_out, sems.at[0]),
-        pltpu.make_async_copy(b_ref, b_out, sems.at[1]),
+def copy_kernel(a_ref, b_ref, a_out, b_out):
+    a_out[...] = a_ref[...]
+    b_out[...] = b_ref[...]
+
+
+def copied(a, b):
+    specs = [
+        pl.BlockSpec((a.shape[0] // 2, a.shape[1]), lambda i: (i, 0)),
+        pl.BlockSpec((1, b.shape[1] // 2) + b.shape[2:], lambda i: (0, i, 0, 0)),
     ]
-    for copy in copies:
-        copy.start()
-    for copy in copies:
-        copy.wait()
-
-
-def copied(a, b):
-    anywhere = pl.BlockSpec(memory_space=pl.ANY)
     return pl.pallas_call(
         copy_kernel,
-        in_specs=[anywhere, anywhere],
-        out_specs=[anywhere, anywhere],
+        grid=(2,),
+        in_specs=specs,
+        out_specs=specs,
         out_shape=[jax.ShapeDtypeStruct(a.shape, a.dtype), jax.ShapeDtypeStruct(b.shape, b.dtype)],
-        scratch_shapes=[pltpu.SemaphoreType.DMA((2,))],
         compiler_params=pltpu.CompilerParams(vmem_limit_bytes=60 * 1024 * 1024),
     )(a, b)
 

time: 111 us -> 80.1 us (0.72)
  Pallas kernels: 110 us -> 79.3 us
    pallas_call x1, Pallas kernels: 32.9 us -> 2.04 us  [copied(): pl.pallas_call(copy_kernel, grid=(2,), in_specs=specs, out_specs=specs, o...]
where the time goes in v6:
time: 80.1 us; the launch traced here: 80 us
  Pallas kernels  79.3 us (99%)
    pallas_call x1, Pallas kernels, tail_part(): pl.pallas_call(functools.partial(tail_kernel, heads, prompts, devices, gr...  53.9 us
    pallas_call x1, Pallas kernels, local_part(): pl.pallas_call(functools.partial(local_kernel, repeat, prompts), grid=(gr...  23.4 us
    pallas_call x1, Pallas kernels, copied(): pl.pallas_call(copy_kernel, grid=(2,), in_specs=specs, out_specs=specs, o...  2.04 us

profile of v6, /device:TPU:0, one launch (start us, length us, event | category | flops | bytes accessed | tf_op | source)
XLA Modules:
  0.0 80.0 jit_solution(6497467916037750334)
XLA Ops:
  0.6 23.4 %shard_map.104 = (f32[512,1024]{1,0:T(8,128)}, bf16[512,1024]{1,0:T(8,128)(2,1)}, f32[8,128,128]{2,1,0:T(8,128)}, bf16[8,128,128]{2,1,0:T(8,128)(2,1)}, f32[4,8,...) custom-call(s32[4]{0:T(128)} %ps_ref.1, s32[4]{0:T(128)} %owner_ref.1, ...), custom_call_target="tpu_custom_call" | custom-call | tf_op jit(solution)/shard_map/pallas_call | solution.py:213
  24.0 53.9 %shard_map.105 = (bf16[512,512]{1,0:T(8,128)(2,1)}, f32[1,8,128,128]{3,2,1,0:T(8,128)}) custom-call(f32[8,128,128]{2,1,0:T(8,128)} %get-tuple-element.11.l_hbm, bf16[8,128,128]{2,1,0:T(8,128)(2,1)} %get-tuple-element.12.m_hbm, f32[8,1,128]{2,1,0:T(1,128)} %get-tuple-element.13.mask_hbm, f32[1,128]{1,0:T(1,128)} %bitcast.1, ...), custom_call_target="tpu_custom_call" | custom-call | tf_op jit(solution)/shard_map/pallas_call | solution.py:552
  77.9 2.0 %shard_map.106 = (bf16[512,512]{1,0:T(8,128)(2,1)}, f32[1,8,128,128]{3,2,1,0:T(8,128)}) custom-call(bf16[512,512]{1,0:T(8,128)(2,1)} %get-tuple-element.18.a_ref, f32[1,8,128,128]{3,2,1,0:T(8,128)} %get-tuple-element.19.b_ref), custom_call_target="tpu_custom_call" | custom-call | tf_op jit(solution)/shard_map/pallas_call | solution.py:597
